TPU v7x, 512 devices: a whole 4x4x16 slice. The times are simulated.
512 devices in a mesh: ctx: 64 (over z, x_hi, core), tp: 8 (over y, x_lo).
Axes of the slice: x: 4 (x_hi: 2, x_lo: 2; x = x_hi * 2 + x_lo), y: 4, z: 16, core: 2. Of those that a mesh axis runs over, the one named last changes fastest.
Arguments:
- qkv_in: bfloat16 [8192, 3, 4096], P('ctx', None, 'tp'), may hold values from -6 to 6
- short_taps: float32 [3, 3, 4096], P(None, None, 'tp'), may hold values from -3.5 to 3.5
- long_filter: float32 [8192, 4096], P('ctx', 'tp'), may hold values from -1.7 to 1.7
- skip_gain: float32 [4096], P('tp'), may hold values from 0.2 to 1.5
- out_weight: bfloat16 [4096, 4096], P('tp', 'ctx'), may hold values from -0.25 to 0.25
Outputs:
- mixed_out: bfloat16 [8192, 4096], P('ctx', 'tp')
All inputs are finite; a program needn't handle non-finite values.
Results may differ from a plain program's by a relative error of at most 0.0049.
Values may be sent and summed in bfloat16 or wider, within the bound.
A program may use at most 64 MiB of HBM per device.

v0:
```python
import math

import jax
import jax.numpy as jnp
from jax import lax
from jax.sharding import PartitionSpec as P

highest = lax.Precision.HIGHEST


def from_behind(value, axis, by):
    length = lax.axis_size(axis)
    pairs = [(i, i + by) for i in range(length) if 0 <= i + by < length]
    return lax.ppermute(value, axis, pairs)


def angles(count_rows, count_cols, offset, period, direction):
    row_ids = lax.iota(jnp.int32, count_rows)[:, None]
    col_ids = lax.iota(jnp.int32, count_cols)[None, :] + offset
    phase_int = row_ids * col_ids % period
    radians = phase_int.astype(jnp.float32) * (direction * 2.0 * math.pi / period)
    return (jnp.cos(radians), jnp.sin(radians))


def across_forward(signal, peer_count):
    cos_table, sin_table = angles(2 * peer_count, peer_count, 0, 2 * peer_count, -1.0)
    real_part = jnp.dot(cos_table, signal, precision=highest, preferred_element_type=jnp.float32)
    imag_part = jnp.dot(sin_table, signal, precision=highest, preferred_element_type=jnp.float32)
    return (real_part, imag_part)


def across_inverse(real_part, imag_part, peer_count):
    cos_table, sin_table = angles(peer_count, 2 * peer_count, 0, 2 * peer_count, 1.0)
    first_term = jnp.dot(
        cos_table, real_part, precision=highest, preferred_element_type=jnp.float32
    )
    second_term = jnp.dot(
        sin_table, imag_part, precision=highest, preferred_element_type=jnp.float32
    )
    return first_term - second_term


def rotate(real_part, imag_part, offset, total_len, direction):
    cos_table, sin_table = angles(
        real_part.shape[0], real_part.shape[1], offset, total_len, direction
    )
    cos_table = cos_table[:, :, None]
    sin_table = sin_table[:, :, None]
    return (
        real_part * cos_table - imag_part * sin_table,
        real_part * sin_table + imag_part * cos_table,
    )


def contract(matrix, operand):
    return jnp.einsum("ki,aic->akc", matrix, operand, precision=highest)


def along_rows(real_part, imag_part, direction):
    row_count = real_part.shape[1]
    cos_table, sin_table = angles(row_count, row_count, 0, row_count, direction)
    new_real = contract(cos_table, real_part) - contract(sin_table, imag_part)
    new_imag = contract(cos_table, imag_part) + contract(sin_table, real_part)
    return (new_real, new_imag)


def multiply(left_pair, right_pair):
    return (
        left_pair[0] * right_pair[0] - left_pair[1] * right_pair[1],
        left_pair[0] * right_pair[1] + left_pair[1] * right_pair[0],
    )


def over_slabs(mixed_in, long_filter):
    peer_count = lax.axis_size("ctx")
    position = lax.axis_index("ctx")
    row_count, channel_count = mixed_in.shape
    block_rows = row_count // peer_count
    total_len = 2 * peer_count * row_count
    pieces_in = (
        lax.all_to_all(mixed_in[None], "ctx", split_axis=1, concat_axis=0, tiled=True),
        lax.all_to_all(long_filter[None], "ctx", split_axis=1, concat_axis=0, tiled=True),
    )
    halves = []
    for received in pieces_in:
        real_part, imag_part = across_forward(
            received.reshape(peer_count, block_rows * channel_count), peer_count
        )
        cube_shape = (2 * peer_count, block_rows, channel_count)
        halves.append(
            rotate(
                real_part.reshape(cube_shape),
                imag_part.reshape(cube_shape),
                position * block_rows,
                total_len,
                -1.0,
            )
        )
    shuffled = (
        lax.all_to_all(halves[0][0], "ctx", split_axis=0, concat_axis=1, tiled=True),
        lax.all_to_all(halves[0][1], "ctx", split_axis=0, concat_axis=1, tiled=True),
        lax.all_to_all(halves[1][0], "ctx", split_axis=0, concat_axis=1, tiled=True),
        lax.all_to_all(halves[1][1], "ctx", split_axis=0, concat_axis=1, tiled=True),
    )
    signal_freq = along_rows(shuffled[0], shuffled[1], -1.0)
    filter_freq = along_rows(shuffled[2], shuffled[3], -1.0)
    product_pair = multiply(signal_freq, filter_freq)
    back_real, back_imag = along_rows(product_pair[0], product_pair[1], 1.0)
    returned = (
        lax.all_to_all(back_real, "ctx", split_axis=1, concat_axis=0, tiled=True),
        lax.all_to_all(back_imag, "ctx", split_axis=1, concat_axis=0, tiled=True),
    )
    turned_real, turned_imag = rotate(
        returned[0], returned[1], position * block_rows, total_len, 1.0
    )
    flat_shape = (2 * peer_count, block_rows * channel_count)
    output = across_inverse(
        turned_real.reshape(flat_shape), turned_imag.reshape(flat_shape), peer_count
    ) * (1.0 / total_len)
    settled = lax.all_to_all(
        output.reshape(peer_count, block_rows, channel_count),
        "ctx",
        split_axis=0,
        concat_axis=1,
        tiled=True,
    )
    return settled.reshape(row_count, channel_count)


def body(qkv_in, short_taps, long_filter, skip_gain, out_weight):
    row_count = qkv_in.shape[0]
    tap_count = short_taps.shape[1]
    last_rows = qkv_in[row_count - (tap_count - 1) :]
    earlier = from_behind(last_rows, "ctx", 1)
    extended = jnp.concatenate([earlier, qkv_in], axis=0).astype(jnp.float32)
    featured = short_taps[:, 0, :][None] * extended[tap_count - 1 : tap_count - 1 + row_count]
    for index_tap in range(1, tap_count):
        begin = tap_count - 1 - index_tap
        featured = (
            featured + short_taps[:, index_tap, :][None] * extended[begin : begin + row_count]
        )
    queries = featured[:, 0, :]
    mixed_in = featured[:, 1, :] * featured[:, 2, :]
    convolved = over_slabs(mixed_in, long_filter)
    gated_rows = (queries * (convolved + skip_gain[None, :] * mixed_in)).astype(jnp.bfloat16)
    partials = jnp.dot(
        gated_rows,
        lax.all_gather(out_weight, "ctx", axis=1, tiled=True),
        preferred_element_type=jnp.float32,
    )
    return lax.psum_scatter(partials, "tp", scatter_dimension=1, tiled=True).astype(jnp.bfloat16)


def solution(mesh):
    return jax.shard_map(
        body,
        mesh=mesh,
        in_specs=(
            P("ctx", None, "tp"),
            P(None, None, "tp"),
            P("ctx", "tp"),
            P("tp"),
            P("tp", "ctx"),
        ),
        out_specs=P("ctx", "tp"),
        check_vma=False,
    )
```

profile of v0, /device:TPU:1, one launch (start us, length us, event | category | flops | bytes accessed | tf_op | source)
XLA Modules:
  0.0 445.4 jit_solution(16840194042781919563)
XLA Ops:
  7.3 6.0 %collective-permute-start = (bf16[2,3,512]{2,0,1:T(2,128)(2,1)S(1)}, bf16[2,3,512]{2,0,1:T(2,128)(2,1)S(1)}, u32[]{:S(2)}, u32[]{:S(2)}) collective-permute-start(bf16[2,3,512]{2,0,1:T(2,128)(2,1)S(1)} %slice.31), channel_id=1, source_target_pairs={{0,8},{8,16},{16,24},{24,32},{32,40},{40,48},{48,56},{56,64},{64,7... | collective-permute-start | bytes 18440 | tf_op jit(solution)/shard_map/ppermute | solution.py:14
  13.3 1.8 broadcast_in_dim.2
  15.2 16.2 %all-to-all-start.3 = ((f32[1,128,512]{2,0,1:T(1,128)}), f32[1,128,512]{2,0,1:T(1,128)S(1)}, u32[]{:S(2)}, u32[]{:S(2)}) async-start(f32[1,128,512]{2,0,1:T(1,128)} %broadcast_in_dim.2), calls=%async_computation.3 | async-start | bytes 524288 | tf_op jit(solution)/shard_map/all_to_all | solution.py:82
  34.8 20.4 %all-to-all-done.3 = f32[1,128,512]{2,0,1:T(1,128)S(1)} async-done(((f32[1,128,512]{2,0,1:T(1,128)}), f32[1,128,512]{2,0,1:T(1,128)S(1)}, u32[]{:S(2)}, u32[]{:S(2)}) %all-to-all-start.3) | async-done | bytes 262176 | tf_op jit(solution)/shard_map/all_to_all | solution.py:82
  55.1 4.2 all-to-all-start
  60.9 21.9 %all-to-all-done = f32[1,128,512]{2,0,1:T(1,128)S(1)} async-done(((f32[1,128,512]{2,0,1:T(1,128)}), f32[1,128,512]{2,0,1:T(1,128)S(1)}, u32[]{:S(2)}, u32[]{:S(2)}) %all-to-all-start) | async-done | bytes 262176 | tf_op jit(solution)/shard_map/all_to_all | solution.py:81
  87.2 4.2 all-to-all-start.4
  91.5 1.2 copy.49
  92.7 32.5 %all-to-all-done.4 = f32[128,2,512]{2,1,0:T(2,128)S(1)} async-done(((f32[128,2,512]{2,1,0:T(2,128)}), f32[128,2,512]{2,1,0:T(2,128)S(1)}, u32[]{:S(2)}, u32[]{:S(2)}) %all-to-all-start.4) | async-done | bytes 524320 | tf_op jit(solution)/shard_map/all_to_all | solution.py:102
  125.2 5.0 %all-to-all-start.5 = ((f32[128,2,512]{2,1,0:T(2,128)}), f32[128,2,512]{2,1,0:T(2,128)S(1)}, u32[]{:S(2)}, u32[]{:S(2)}) async-start(f32[128,2,512]{2,1,0:T(2,128)} %copy.49), calls=%async_computation.5 | async-start | bytes 1048576 | tf_op jit(solution)/shard_map/all_to_all | solution.py:103
  131.3 32.8 %all-to-all-done.5 = f32[128,2,512]{2,1,0:T(2,128)S(1)} async-done(((f32[128,2,512]{2,1,0:T(2,128)}), f32[128,2,512]{2,1,0:T(2,128)S(1)}, u32[]{:S(2)}, u32[]{:S(2)}) %all-to-all-start.5) | async-done | bytes 524320 | tf_op jit(solution)/shard_map/all_to_all | solution.py:103
  164.2 5.0 %all-to-all-start.1 = ((f32[128,2,512]{2,1,0:T(2,128)}), f32[128,2,512]{2,1,0:T(2,128)S(1)}, u32[]{:S(2)}, u32[]{:S(2)}) async-start(f32[128,2,512]{2,1,0:T(2,128)} %copy.38), calls=%async_computation.1 | async-start | bytes 1048576 | tf_op jit(solution)/shard_map/all_to_all | solution.py:100
  170.3 32.8 %all-to-all-done.1 = f32[128,2,512]{2,1,0:T(2,128)S(1)} async-done(((f32[128,2,512]{2,1,0:T(2,128)}), f32[128,2,512]{2,1,0:T(2,128)S(1)}, u32[]{:S(2)}, u32[]{:S(2)}) %all-to-all-start.1) | async-done | bytes 524320 | tf_op jit(solution)/shard_map/all_to_all | solution.py:100
  203.1 5.0 %all-to-all-start.2 = ((f32[128,2,512]{2,1,0:T(2,128)}), f32[128,2,512]{2,1,0:T(2,128)S(1)}, u32[]{:S(2)}, u32[]{:S(2)}) async-start(f32[128,2,512]{2,1,0:T(2,128)} %copy.41), calls=%async_computation.2 | async-start | bytes 1048576 | tf_op jit(solution)/shard_map/all_to_all | solution.py:101
  210.4 31.7 %all-to-all-done.2 = f32[128,2,512]{2,1,0:T(2,128)S(1)} async-done(((f32[128,2,512]{2,1,0:T(2,128)}), f32[128,2,512]{2,1,0:T(2,128)S(1)}, u32[]{:S(2)}, u32[]{:S(2)}) %all-to-all-start.2) | async-done | bytes 524320 | tf_op jit(solution)/shard_map/all_to_all | solution.py:101
  251.9 5.2 %all-to-all-start.6 = ((f32[2,128,512]{2,0,1:T(2,128)}), f32[2,128,512]{2,0,1:T(2,128)S(1)}, u32[]{:S(2)}, u32[]{:S(2)}) async-start(f32[2,128,512]{2,0,1:T(2,128)} %copy.56), calls=%async_computation.6 | async-start | bytes 1048576 | tf_op jit(solution)/shard_map/all_to_all | solution.py:110
  259.8 32.6 %all-to-all-done.6 = f32[2,128,512]{2,0,1:T(2,128)S(1)} async-done(((f32[2,128,512]{2,0,1:T(2,128)}), f32[2,128,512]{2,0,1:T(2,128)S(1)}, u32[]{:S(2)}, u32[]{:S(2)}) %all-to-all-start.6) | async-done | bytes 524320 | tf_op jit(solution)/shard_map/all_to_all | solution.py:110
  292.4 5.6 %all-to-all-start.7 = ((f32[2,128,512]{2,0,1:T(2,128)}), f32[2,128,512]{2,0,1:T(2,128)S(1)}, u32[]{:S(2)}, u32[]{:S(2)}) async-start(f32[2,128,512]{2,0,1:T(2,128)} %copy.59), calls=%async_computation.7 | async-start | bytes 1048576 | tf_op jit(solution)/shard_map/all_to_all | solution.py:111
  299.3 34.2 %all-to-all-done.7 = f32[2,128,512]{2,0,1:T(2,128)S(1)} async-done(((f32[2,128,512]{2,0,1:T(2,128)}), f32[2,128,512]{2,0,1:T(2,128)S(1)}, u32[]{:S(2)}, u32[]{:S(2)}) %all-to-all-start.7) | async-done | bytes 524320 | tf_op jit(solution)/shard_map/all_to_all | solution.py:111
  335.3 29.8 %all_to_all.135 = f32[64,2,512]{2,1,0:T(2,128)S(1)} all-to-all(f32[64,2,512]{2,1,0:T(2,128)S(1)} %reshape.160), channel_id=1, replica_groups=mesh['ctx'=64,'tp'=8] {'ctx'}, dimensions={0} | all-to-all | bytes 524288 | tf_op jit(solution)/shard_map/all_to_all | solution.py:120
  365.3 11.9 %all-gather.2.cloned.1.call-done = bf16[512,4096]{0,1:T(8,128)(2,1)} async-done(((bf16[512,64]{0,1:T(8,128)(2,1)}), bf16[512,4096]{0,1:T(8,128)(2,1)}) %all-gather.2.cloned.1.call-update) | async-done | bytes 4194320 | tf_op jit(solution)/shard_map/all_gather | solution.py:148
  377.3 5.1 %fusion.33 = f32[128,4096]{1,0:T(8,128)} fusion(bf16[512,4096]{0,1:T(8,128)(2,1)} %all-gather.2.cloned.1.call-done, f32[128,3,512]{2,0,1:T(8,128)S(1)} %fusion.3, f32[128,512]{1,0:T(8,128)S(1)} %reshape.161, f32[128,1,512]{2,1,0:T(1,128)} %copy_multiply_fusion, f32[512]{0:T(512)S(1)} %copy-done), kind=kOutput, calls=%fused_computation.53 | convolution fusion | flops 537133056 | bytes 7079936 | tf_op jit(solution)/shard_map/dot_general | solution.py:146
  382.4 54.5 %reduce-scatter.2.cloned.1.call-done = f32[128,512]{1,0:T(8,128)} async-done(((f32[128,4096]{1,0:T(8,128)}), f32[128,512]{1,0:T(8,128)}) %reduce-scatter.2.cloned.1.call-update) | async-done | bytes 262160 | tf_op jit(solution)/shard_map/reduce_scatter | solution.py:151
  436.9 1.6 convert_element_type.75
  (64 shorter events, 30.2 us)
Async XLA Ops:
  7.3 24.9 %collective-permute-start = (bf16[2,3,512]{2,0,1:T(2,128)(2,1)S(1)}, bf16[2,3,512]{2,0,1:T(2,128)(2,1)S(1)}, u32[]{:S(2)}, u32[]{:S(2)}) collective-permute-start(bf16[2,3,512]{2,0,1:T(2,128)(2,1)S(1)} %slice.31), channel_id=1, source_target_pairs={{0,8},{8,16},{16,24},{24,32},{32,40},{40,48},{48,56},{56,64},{64,7... | collective-permute-start | bytes 18440 | tf_op jit(solution)/shard_map/ppermute | solution.py:14
  15.2 40.0 %all-to-all-start.3 = ((f32[1,128,512]{2,0,1:T(1,128)}), f32[1,128,512]{2,0,1:T(1,128)S(1)}, u32[]{:S(2)}, u32[]{:S(2)}) async-start(f32[1,128,512]{2,0,1:T(1,128)} %broadcast_in_dim.2), calls=%async_computation.3 | async-start | bytes 524288 | tf_op jit(solution)/shard_map/all_to_all | solution.py:82
  55.1 27.8 %all-to-all-start = ((f32[1,128,512]{2,0,1:T(1,128)}), f32[1,128,512]{2,0,1:T(1,128)S(1)}, u32[]{:S(2)}, u32[]{:S(2)}) async-start(f32[1,128,512]{2,0,1:T(1,128)} %bitcast.2), calls=%async_computation | async-start | bytes 524288 | tf_op jit(solution)/shard_map/all_to_all | solution.py:81
  87.2 37.9 %all-to-all-start.4 = ((f32[128,2,512]{2,1,0:T(2,128)}), f32[128,2,512]{2,1,0:T(2,128)S(1)}, u32[]{:S(2)}, u32[]{:S(2)}) async-start(f32[128,2,512]{2,1,0:T(2,128)} %copy.46), calls=%async_computation.4 | async-start | bytes 1048576 | tf_op jit(solution)/shard_map/all_to_all | solution.py:102
  125.2 39.0 %all-to-all-start.5 = ((f32[128,2,512]{2,1,0:T(2,128)}), f32[128,2,512]{2,1,0:T(2,128)S(1)}, u32[]{:S(2)}, u32[]{:S(2)}) async-start(f32[128,2,512]{2,1,0:T(2,128)} %copy.49), calls=%async_computation.5 | async-start | bytes 1048576 | tf_op jit(solution)/shard_map/all_to_all | solution.py:103
  164.2 39.0 %all-to-all-start.1 = ((f32[128,2,512]{2,1,0:T(2,128)}), f32[128,2,512]{2,1,0:T(2,128)S(1)}, u32[]{:S(2)}, u32[]{:S(2)}) async-start(f32[128,2,512]{2,1,0:T(2,128)} %copy.38), calls=%async_computation.1 | async-start | bytes 1048576 | tf_op jit(solution)/shard_map/all_to_all | solution.py:100
  203.1 39.0 %all-to-all-start.2 = ((f32[128,2,512]{2,1,0:T(2,128)}), f32[128,2,512]{2,1,0:T(2,128)S(1)}, u32[]{:S(2)}, u32[]{:S(2)}) async-start(f32[128,2,512]{2,1,0:T(2,128)} %copy.41), calls=%async_computation.2 | async-start | bytes 1048576 | tf_op jit(solution)/shard_map/all_to_all | solution.py:101
  208.1 169.2 %all-gather.2.cloned.1.call-start = ((), (), s32[]{:S(2)}) async-start(), calls=%async_computation.10 | async-start | bytes 4259840 | tf_op jit(solution)/shard_map/all_gather | solution.py:148
  251.9 40.6 %all-to-all-start.6 = ((f32[2,128,512]{2,0,1:T(2,128)}), f32[2,128,512]{2,0,1:T(2,128)S(1)}, u32[]{:S(2)}, u32[]{:S(2)}) async-start(f32[2,128,512]{2,0,1:T(2,128)} %copy.56), calls=%async_computation.6 | async-start | bytes 1048576 | tf_op jit(solution)/shard_map/all_to_all | solution.py:110
  292.4 41.1 %all-to-all-start.7 = ((f32[2,128,512]{2,0,1:T(2,128)}), f32[2,128,512]{2,0,1:T(2,128)S(1)}, u32[]{:S(2)}, u32[]{:S(2)}) async-start(f32[2,128,512]{2,0,1:T(2,128)} %copy.59), calls=%async_computation.7 | async-start | bytes 1048576 | tf_op jit(solution)/shard_map/all_to_all | solution.py:111
  298.0 138.9 %reduce-scatter.2.cloned.1.call-start = ((), (), s32[]{:S(2)}) async-start(), calls=%async_computation.11 | async-start | bytes 2359296 | tf_op jit(solution)/shard_map/reduce_scatter | solution.py:151
  333.5 43.7 %copy-start = (f32[512]{0:T(512)S(1)}, f32[512]{0:T(512)}, u32[]{:S(2)}) copy-start(f32[512]{0:T(512)} %param.8) | copy-start | bytes 6148
Sparse Core Ops, SparseCore 0:
  212.2 165.0 all-gather.1
  382.5 54.3 reduce-scatter.1
where the time goes:
time: 446 us; the launch traced here: 445 us
  waiting for transfers between devices  306 us (69%)
  starting transfers between devices  56.3 us (13%)
  blocking collectives  29.8 us (7%)
  matrix products  19.4 us (4%)
  local copies, waits for them, and re-layouts  14.4 us (3%)
  between operations  13.8 us (3%)
  other arithmetic  5.45 us (1%)
    reduce_scatter x1, waiting for transfers between devices, body(): lax.psum_scatter(partials, 'tp', scatter_dimension=1, tiled=True)  54.5 us
    all_to_all x1, waiting for transfers between devices, over_slabs(): lax.all_to_all(back_imag, 'ctx', split_axis=1, concat_axis=0, tiled=True)  34.2 us
    all_to_all x1, waiting for transfers between devices, over_slabs(): lax.all_to_all(halves[1][1], 'ctx', split_axis=0, concat_axis=1, tiled=True)  32.8 us
    all_to_all x1, waiting for transfers between devices, over_slabs(): lax.all_to_all(halves[0][0], 'ctx', split_axis=0, concat_axis=1, tiled=True)  32.8 us
    all_to_all x1, waiting for transfers between devices, over_slabs(): lax.all_to_all(back_real, 'ctx', split_axis=1, concat_axis=0, tiled=True)  32.6 us
    all_to_all x1, waiting for transfers between devices, over_slabs(): lax.all_to_all(halves[1][0], 'ctx', split_axis=0, concat_axis=1, tiled=True)  32.5 us
    all_to_all x1, waiting for transfers between devices, over_slabs(): lax.all_to_all(halves[0][1], 'ctx', split_axis=0, concat_axis=1, tiled=True)  31.7 us
    all_to_all x1, blocking collectives, over_slabs(): lax.all_to_all(output.reshape(peer_count, block_rows, channel_count), 'ct...  29.8 us
  transfers between devices with their start and end apart: 11, of which 10 were waited for; matrix products, arithmetic and copies ran while one was open for 6% of the time, Pallas kernels for 0%

commit v1 on v0

v1 whole, which is shorter than its diff:
```python
import functools

import jax
import jax.numpy as jnp
import numpy as np
from jax import lax
from jax.experimental import pallas as pl
from jax.experimental.pallas import tpu as pltpu
from jax.sharding import Mesh, PartitionSpec as P

F32 = jnp.float32
BF16 = jnp.bfloat16
CH = 8
VMEM = pl.BlockSpec(memory_space=pltpu.VMEM)


def split_hi_lo(table):
    high = table.astype(np.float32).astype(jnp.bfloat16)
    low = (table - high.astype(np.float64)).astype(np.float32).astype(jnp.bfloat16)
    return high, low


def tables(blocks, width):
    length = blocks * width
    f1 = np.arange(blocks)[:, None]
    a = np.exp(-2j * np.pi * ((np.arange(blocks)[None, :] * (4 * f1 + 1)) % (4 * blocks)) / (4 * blocks))
    t = np.exp(-2j * np.pi * (np.arange(width)[None, :] * (4 * f1 + 1)) / (4 * length))
    i = np.arange(width)
    b = np.exp(-2j * np.pi * ((i[:, None] * i[None, :]) % width) / width)
    a_high, a_low = split_hi_lo(np.concatenate([a.real, a.imag], 0))
    b_high, b_low = split_hi_lo(np.block([[b.real, b.imag], [-b.imag, b.real]]))
    c_high, c_low = split_hi_lo(np.block([[b.real, -b.imag], [b.imag, b.real]]))
    d_high, d_low = split_hi_lo(np.concatenate([a.real.T, a.imag.T], 1) / length)
    return (
        np.concatenate([a_high, a_low], 1),
        t.real.astype(np.float32),
        t.imag.astype(np.float32),
        np.concatenate([b_high, b_high, b_low], 0),
        np.concatenate([c_high, c_high, c_low], 0),
        np.concatenate([d_high, d_high, d_low], 1),
    )


def dot(left, right):
    return jnp.dot(left, right, preferred_element_type=F32)


def high_low(value):
    high = value.astype(BF16)
    return high, (value - high.astype(F32)).astype(BF16)


def send_all(chips, me, source, target, send_sem, recv_sem):
    def step(k, carry):
        peer = lax.rem(me + k, chips)
        pltpu.make_async_remote_copy(
            src_ref=source.at[peer],
            dst_ref=target.at[me],
            send_sem=send_sem,
            recv_sem=recv_sem,
            device_id={"z": peer // 2, "xh": lax.rem(peer, 2)},
        ).start()
        return carry

    lax.fori_loop(1, chips, step, 0)
    target[pl.ds(me, 1)] = source[pl.ds(me, 1)]


def wait_all(chips, ref, sem):
    part = ref.at[pl.ds(0, chips - 1)]
    pltpu.make_async_copy(part, part, sem).wait()


def spectrum(received, scratch, a_fwd, t_re, t_im, b_fwd):
    rows = scratch.shape[0]
    blocks = rows // CH
    scratch[...] = received[...].astype(F32).reshape(rows, -1)
    columns = [scratch[pl.ds(c, blocks, stride=CH), :].astype(BF16) for c in range(CH)]
    signal = jnp.concatenate(columns, axis=1)
    mixed = dot(a_fwd[...], jnp.concatenate([signal, signal], axis=0))
    width = t_re.shape[1]
    parts = []
    for c in range(CH):
        re = mixed[:blocks, c * width : (c + 1) * width]
        im = mixed[blocks:, c * width : (c + 1) * width]
        parts.append(
            jnp.concatenate(
                [re * t_re[...] - im * t_im[...], re * t_im[...] + im * t_re[...]], axis=1
            )
        )
    high, low = high_low(jnp.concatenate(parts, axis=0))
    return dot(jnp.concatenate([high, low, high], axis=1), b_fwd[...])


def inverse(product, scratch, t_re, t_im, b_inv, a_inv):
    blocks, width = t_re.shape
    high, low = high_low(product)
    back = dot(jnp.concatenate([high, low, high], axis=1), b_inv[...])
    parts = []
    for c in range(CH):
        re = back[c * blocks : (c + 1) * blocks, :width]
        im = back[c * blocks : (c + 1) * blocks, width:]
        parts.append(
            jnp.concatenate(
                [re * t_re[...] + im * t_im[...], im * t_re[...] - re * t_im[...]], axis=0
            )
        )
    high, low = high_low(jnp.concatenate(parts, axis=1))
    result = dot(a_inv[...], jnp.concatenate([high, low, high], axis=0))
    for c in range(CH):
        scratch[pl.ds(c, blocks, stride=CH), :] = result[:, c * width : (c + 1) * width]


def conv_kernel(
    chips,
    qkv, taps, filt, skip, a_fwd, t_re, t_im, b_fwd, b_inv, a_inv,
    gated,
    h_own, h_pair, h_send, h_recv, x_all, u_send, u_recv, y_send, y_recv, scratch,
    near_send, near_recv, far_send, far_recv, local_sem,
):
    core = lax.axis_index("core")
    me = lax.axis_index("z") * 2 + lax.axis_index("xh")
    other = 1 - core
    rows = qkv.shape[1]
    half = chips * CH
    halo = 16

    barrier = pltpu.get_barrier_semaphore()
    pl.semaphore_signal(barrier, inc=1, device_id={"core": other})
    step_to = lax.rem(me + jnp.where(core == 1, 1, chips - 1), chips)
    pl.semaphore_signal(
        barrier, inc=1, device_id={"z": step_to // 2, "xh": lax.rem(step_to, 2), "core": other}
    )

    def greet(k, carry):
        peer = lax.rem(me + k, chips)
        pl.semaphore_signal(
            barrier, inc=1, device_id={"z": peer // 2, "xh": lax.rem(peer, 2)}
        )
        return carry

    lax.fori_loop(1, chips, greet, 0)

    turned = filt[...].T.reshape(2, chips, CH, rows)
    h_own[...] = turned
    pl.semaphore_wait(barrier, chips + 1)

    my_rows = pl.ds(pl.multiple_of(core * CH, CH), CH)
    h_copy = pltpu.make_async_remote_copy(
        src_ref=h_own.at[other],
        dst_ref=h_pair.at[:, my_rows, :],
        send_sem=near_send.at[0],
        recv_sem=near_recv.at[0],
        device_id={"core": other},
    )
    h_copy.start()
    mine = pl.ds(pl.multiple_of(core * half, half), half)
    theirs = pl.ds(pl.multiple_of(other * half, half), half)
    place = pl.ds(pl.multiple_of(halo + core * rows, 16), rows)
    x_copy = pltpu.make_async_remote_copy(
        src_ref=qkv.at[:, :, theirs],
        dst_ref=x_all.at[:, place, :],
        send_sem=near_send.at[1],
        recv_sem=near_recv.at[1],
        device_id={"core": other},
    )
    x_copy.start()

    after = lax.rem(me + 1, chips)

    def halo_copy(target):
        return pltpu.make_async_remote_copy(
            src_ref=qkv.at[:, pl.ds(rows - halo, halo), pl.ds(target * half, half)],
            dst_ref=x_all.at[:, pl.ds(0, halo), :],
            send_sem=near_send.at[2 + target],
            recv_sem=near_recv.at[2],
            device_id={"z": after // 2, "xh": lax.rem(after, 2), "core": target},
        )

    @pl.when(core == 1)
    def _():
        halo_copy(0).start()
        halo_copy(1).start()

    x_local = pltpu.make_async_copy(qkv.at[:, :, mine], x_all.at[:, place, :], local_sem)
    x_local.start()
    h_pair[:, my_rows, :] = h_own[pl.ds(core, 1)].reshape(chips, CH, rows)
    h_copy.wait_recv()
    h_send[...] = h_pair[...].astype(BF16)
    send_all(chips, me, h_send, h_recv, far_send.at[0], far_recv.at[0])

    x_local.wait()
    x_copy.wait_recv()
    halo_copy(0).wait_recv()

    @pl.when(core == 1)
    def _():
        halo_copy(0).wait_send()
        halo_copy(1).wait_send()

    features = []
    for s in range(3):
        x = x_all[s].astype(F32)
        first = jnp.where(me == 0, 0.0, x[:halo])
        x = jnp.concatenate([first, x[halo:]], axis=0)
        total = taps[s, 0:1, mine] * x[halo:]
        for back in range(1, taps.shape[1]):
            total = total + taps[s, back : back + 1, mine] * x[halo - back : halo - back + 2 * rows]
        features.append(total)
    query, mixed_in = features[0], features[1] * features[2]
    flipped = mixed_in.T.reshape(chips, CH, 2 * rows)
    u_send[...] = jnp.concatenate([flipped[:, :, :rows], flipped[:, :, rows:]], axis=1).astype(BF16)
    send_all(chips, me, u_send, u_recv, far_send.at[1], far_recv.at[1])

    wait_all(chips, h_recv, far_recv.at[0])
    h_freq = spectrum(h_recv, scratch, a_fwd, t_re, t_im, b_fwd)
    wait_all(chips, u_recv, far_recv.at[1])
    u_freq = spectrum(u_recv, scratch, a_fwd, t_re, t_im, b_fwd)
    width = t_re.shape[1]
    h_re, h_im = h_freq[:, :width], h_freq[:, width:]
    u_re, u_im = u_freq[:, :width], u_freq[:, width:]
    product = jnp.concatenate([h_re * u_re - h_im * u_im, h_re * u_im + h_im * u_re], axis=1)
    inverse(product, scratch, t_re, t_im, b_inv, a_inv)
    y_send[...] = scratch[...].reshape(y_send.shape).astype(BF16)
    send_all(chips, me, y_send, y_recv, far_send.at[2], far_recv.at[2])
    wait_all(chips, y_recv, far_recv.at[2])
    back = y_recv[...].astype(F32)
    convolved = jnp.concatenate(
        [back[:, CH * b : CH * (b + 1), :].reshape(half, rows).T for b in range(2)], axis=0
    )
    gated[...] = (query * (convolved + skip[:, mine] * mixed_in)).astype(BF16)

    h_copy.wait_send()
    x_copy.wait_send()
    wait_all(chips, h_send, far_send.at[0])
    wait_all(chips, u_send, far_send.at[1])
    wait_all(chips, y_send, far_send.at[2])


def project_kernel(
    groups, gated, weight, out, g_all, parts, landed, near_send, near_recv, far_send, far_recv
):
    core, xh = lax.axis_index("core"), lax.axis_index("xh")
    xls = lax.axis_size("xl")
    me = lax.axis_index("y") * xls + lax.axis_index("xl")
    tokens, half = gated.shape
    rows = tokens // 2
    slot = xh * 2 + core

    barrier = pltpu.get_barrier_semaphore()

    def place(index):
        which, owner = index // groups, lax.rem(index, groups)
        return {
            "xh": which // 2,
            "core": lax.rem(which, 2),
            "y": owner // xls,
            "xl": lax.rem(owner, xls),
        }

    everyone = 4 * groups
    my_index = slot * groups + me

    def greet(k, carry):
        pl.semaphore_signal(barrier, inc=1, device_id=place(lax.rem(my_index + k, everyone)))
        return carry

    lax.fori_loop(1, everyone, greet, 0)
    mine = pl.ds(pl.multiple_of(core * half, half), half)
    g_all[pl.ds(xh, 1), :, mine] = gated[...].reshape(1, tokens, half)
    pl.semaphore_wait(barrier, everyone - 1)

    copies = []
    for far in range(2):
        for cross in range(2):
            if far == 0 and cross == 0:
                continue
            index = far * 2 + cross - 1
            copies.append(
                pltpu.make_async_remote_copy(
                    src_ref=gated,
                    dst_ref=g_all.at[xh, :, mine],
                    send_sem=near_send.at[index],
                    recv_sem=near_recv.at[index],
                    device_id={
                        "xh": 1 - xh if far else xh,
                        "core": 1 - core if cross else core,
                    },
                )
            )
    for copy in copies:
        copy.start()

    wide = landed.shape[-1]

    def send(which_x, b, owner):
        pltpu.make_async_remote_copy(
            src_ref=parts.at[which_x, b, owner],
            dst_ref=landed.at[slot, me],
            send_sem=far_send,
            recv_sem=far_recv.at[slot, me],
            device_id={"xh": which_x, "core": b, "y": owner // xls, "xl": lax.rem(owner, xls)},
        ).start()

    def compute(which_x, owner):
        block = weight[pl.ds(pl.multiple_of(owner * wide, wide), wide), :]
        left = g_all[pl.ds(which_x, 1)].reshape(tokens, 2 * half)
        product = lax.dot_general(
            left, block, (((1,), (1,)), ((), ())), preferred_element_type=F32
        ).astype(BF16)
        for b in range(2):
            parts[pl.ds(which_x, 1), b, pl.ds(owner, 1)] = product[
                b * rows : (b + 1) * rows
            ].reshape(1, 1, rows, wide)

    copies[0].wait_recv()

    def own_step(k, carry):
        owner = lax.rem(me + k, groups)
        compute(xh, owner)
        for b in range(2):
            send(xh, b, owner)
        return carry

    lax.fori_loop(1, groups, own_step, 0)
    compute(xh, me)
    send(xh, 1 - core, me)
    landed[pl.ds(slot, 1), pl.ds(me, 1)] = parts[
        pl.ds(xh, 1), pl.ds(core, 1), pl.ds(me, 1)
    ].reshape(1, 1, rows, wide)
    copies[1].wait_recv()
    copies[2].wait_recv()

    def far_step(k, carry):
        owner = lax.rem(me + k, groups)
        compute(1 - xh, owner)
        for b in range(2):
            send(1 - xh, b, owner)
        return carry

    lax.fori_loop(0, groups, far_step, 0)

    def arrived(k, carry):
        index = lax.rem(my_index + k, everyone)
        which, owner = index // groups, lax.rem(index, groups)
        block = landed.at[which, owner]
        pltpu.make_async_copy(block, block, far_recv.at[which, owner]).wait()
        return carry

    lax.fori_loop(1, everyone, arrived, 0)
    sums = []
    for s in range(4):
        total = landed[s, 0].astype(F32)
        for owner in range(1, groups):
            total = total + landed[s, owner].astype(F32)
        sums.append(total)
    width = weight.shape[0] // lax.axis_size("z")
    for part in range(wide // width):
        columns = [total[:, part * width : (part + 1) * width] for total in sums]
        out[:, part * 4 * width : (part + 1) * 4 * width] = jnp.concatenate(
            columns, axis=1
        ).astype(out.dtype)

    for copy in copies:
        copy.wait_send()
    sent = parts.at[0, 0, pl.ds(0, groups - 1)]
    pltpu.make_async_copy(sent, sent, far_send).wait()
    rest = parts.at[0, 1]
    pltpu.make_async_copy(rest, rest, far_send).wait()
    rest = parts.at[1]
    pltpu.make_async_copy(rest, rest, far_send).wait()


def body(qkv_in, short_taps, long_filter, skip_gain, out_weight):
    rows, _, channels = qkv_in.shape
    half = channels // 2
    chips = lax.axis_size("z") * lax.axis_size("xh")
    groups = lax.axis_size("y") * lax.axis_size("xl")
    blocks = 2 * chips
    weight = lax.all_gather(out_weight.T, "z", axis=0, tiled=True)
    lookup = tables(blocks, rows)
    exchange = (chips, 2 * CH, rows)
    gated = pl.pallas_call(
        functools.partial(conv_kernel, chips),
        out_shape=jax.ShapeDtypeStruct((2 * rows, half), BF16),
        in_specs=[VMEM] * 10,
        out_specs=VMEM,
        scratch_shapes=[
            pltpu.VMEM((2, chips, CH, rows), F32),
            pltpu.VMEM(exchange, F32),
            pltpu.VMEM(exchange, BF16),
            pltpu.VMEM(exchange, BF16),
            pltpu.VMEM((3, 16 + 2 * rows, half), BF16),
            pltpu.VMEM(exchange, BF16),
            pltpu.VMEM(exchange, BF16),
            pltpu.VMEM(exchange, BF16),
            pltpu.VMEM(exchange, BF16),
            pltpu.VMEM((blocks * CH, rows), F32),
            pltpu.SemaphoreType.DMA((4,)),
            pltpu.SemaphoreType.DMA((3,)),
            pltpu.SemaphoreType.DMA((3,)),
            pltpu.SemaphoreType.DMA((3,)),
            pltpu.SemaphoreType.DMA,
        ],
        compiler_params=pltpu.CompilerParams(
            collective_id=0, has_side_effects=True, vmem_limit_bytes=32 * 2**20
        ),
        name="conv",
    )(
        qkv_in.transpose(1, 0, 2),
        short_taps,
        long_filter,
        skip_gain[None, :],
        *[jnp.asarray(table) for table in lookup],
    )
    wide = weight.shape[0] // groups
    return pl.pallas_call(
        functools.partial(project_kernel, groups),
        out_shape=jax.ShapeDtypeStruct((rows, channels), BF16),
        in_specs=[VMEM] * 2,
        out_specs=VMEM,
        scratch_shapes=[
            pltpu.VMEM((2, 2 * rows, channels), BF16),
            pltpu.VMEM((2, 2, groups, rows, wide), BF16),
            pltpu.VMEM((4, groups, rows, wide), BF16),
            pltpu.SemaphoreType.DMA((3,)),
            pltpu.SemaphoreType.DMA((3,)),
            pltpu.SemaphoreType.DMA,
            pltpu.SemaphoreType.DMA((4, groups)),
        ],
        compiler_params=pltpu.CompilerParams(
            collective_id=1, has_side_effects=True, vmem_limit_bytes=32 * 2**20
        ),
        name="project",
    )(gated, weight)


def solution(mesh):
    sizes = dict(mesh.shape)
    split = Mesh(
        mesh.devices.reshape(sizes["ctx"] // 4, 2, 2, sizes["tp"] // 2, 2),
        ("z", "xh", "core", "y", "xl"),
    )
    ctx, tp = ("z", "xh", "core"), ("y", "xl")
    return jax.shard_map(
        body,
        mesh=split,
        in_specs=(P(ctx, None, tp), P(None, None, tp), P(ctx, tp), P(tp), P(tp, ctx)),
        out_specs=P(ctx, tp),
        check_vma=False,
    )
```

time: 446 us -> 130 us (0.29)
  waiting for transfers between devices: 306 us -> 20.2 us
  Pallas kernels: 0 us -> 87.4 us
  starting transfers between devices: 56.3 us -> 0.01 us
  blocking collectives: 29.8 us -> 0 us
  matrix products: 19.4 us -> 0 us
  local copies, waits for them, and re-layouts: 14.4 us -> 8.76 us
  other arithmetic: 5.45 us -> 0 us
    all_to_all x8 -> x0, waiting for transfers between devices: 239 us -> none  [the longest x1 34.2 us: over_slabs(): lax.all_to_all(back_imag, 'ctx', split_axis=1, concat_axis=0, tiled=True)]
    pallas_call x0 -> x2, Pallas kernels: none -> 87.4 us  [the longest x1 50.1 us: body(): pl.pallas_call(functools.partial(conv_kernel, chips), out_shape=jax.Shape...]
    reduce_scatter x1 -> x0, waiting for transfers between devices: 54.5 us -> none  [body(): lax.psum_scatter(partials, 'tp', scatter_dimension=1, tiled=True)]
    all_to_all x8 -> x0, starting transfers between devices: 50.2 us -> none  [the longest x1 16.2 us: over_slabs(): lax.all_to_all(long_filter[None], 'ctx', split_axis=1, concat_axis=0, til...]
    all_to_all x1 -> x0, blocking collectives: 29.8 us -> none  [over_slabs(): lax.all_to_all(output.reshape(peer_count, block_rows, channel_count), 'ct...]
    dot_general x19 -> x0, matrix products: 19.4 us -> none  [the longest x12 9.89 us: contract(): return jnp.einsum('ki,aic->akc', matrix, operand, precision=highest)]
    unnamed x8 -> x23, local copies, waits for them, and re-layouts: 0.4 us -> 8.76 us
    all_gather x1, waiting for transfers between devices: 11.9 us -> 19.5 us  [body(): weight = lax.all_gather(out_weight.T, 'z', axis=0, tiled=True)]
  transfers between devices with their start and end apart: 11 -> 1, of which waited for: 10 -> 1; matrix products, arithmetic and copies ran while one was open for 6% -> 0% of each run, Pallas kernels for 0% -> 39%
where the time goes in v1:
time: 130 us
  Pallas kernels  87.4 us (67%)
  waiting for transfers between devices  20.2 us (16%)
  between operations  13.4 us (10%)
  local copies, waits for them, and re-layouts  8.76 us (7%)
    pallas_call x1, Pallas kernels, body(): pl.pallas_call(functools.partial(conv_kernel, chips), out_shape=jax.Shape...  50.1 us
    pallas_call x1, Pallas kernels, body(): pl.pallas_call(functools.partial(project_kernel, groups), out_shape=jax.S...  37.3 us
    all_gather x1, waiting for transfers between devices, body(): weight = lax.all_gather(out_weight.T, 'z', axis=0, tiled=True)  19.5 us
    unnamed x23, local copies, waits for them, and re-layouts  8.76 us
  transfers between devices with their start and end apart: 1, of which 1 were waited for; matrix products, arithmetic and copies ran while one was open for 0% of the time, Pallas kernels for 39%

profile of v1, /device:TPU:1, one launch (start us, length us, event | category | flops | bytes accessed | tf_op | source)
XLA Modules:
  0.0 129.8 jit_solution(10320819684693598469)
XLA Ops:
  6.5 0.0 all-gather.2.cloned.1.call-start
  6.5 0.0 copy-start.6
  6.5 0.7 all-gather.2.cloned.1.call-update
  7.3 0.0 copy-start.10
  7.3 0.1 copy-done.5
  7.3 0.0 copy-done.6
  7.3 0.6 copy-done.10
  8.0 0.0 copy-start.1
  8.0 1.0 copy-done.1
  8.9 0.0 copy-start.2
  8.9 1.0 copy-done.2
  9.9 0.0 copy-start.3
  9.9 1.0 copy-done.3
  10.9 0.0 copy-start.4
  10.9 0.9 copy-done.4
  11.9 0.0 copy-start.7
  11.9 0.8 copy-done.7
  12.7 0.8 copy-done.8
  13.4 0.7 copy-done.9
  14.1 50.1 %conv.1.gated = bf16[256,256]{1,0:T(8,128)(2,1)S(1)} custom-call(bf16[3,128,512]{2,1,0:T(8,128)(2,1)S(1)} %bitcast.3, f32[3,3,512]{2,1,0:T(4,128)S(1)} %copy-done.9, f32[128,512]{1,0:T(8,128)S(1)} %copy-done.4, f32[1,512]{1,0:T(1,128)S(1)} %bitcast.4, bf16[128,128]{1,0:T(8,128)(2,1)S(1)} %copy-done.8, f32[64,128]{1,0:T(8,128)S(1)} %copy-done.7, ...), custom_call_target="tpu_custom_call" | custom-call | tf_op jit(solution)/shard_map/conv/pallas_call | solution.py:383
  64.3 19.5 %all-gather.2.cloned.1.call-done.weight = bf16[1024,512]{1,0:T(8,128)(2,1)} async-done(((bf16[64,512]{1,0:T(8,128)(2,1)}), bf16[1024,512]{1,0:T(8,128)(2,1)}) %all-gather.2.cloned.1.call-update) | async-done | bytes 1048592 | tf_op jit(solution)/shard_map/all_gather | solution.py:380
  83.7 1.2 copy-done
  85.0 37.3 %project.1 = bf16[128,512]{1,0:T(8,128)(2,1)S(1)} custom-call(bf16[256,256]{1,0:T(8,128)(2,1)S(1)} %conv.1.gated, bf16[1024,512]{1,0:T(8,128)(2,1)S(1)} %copy-done), custom_call_target="tpu_custom_call" | custom-call | tf_op jit(solution)/shard_map/project/pallas_call | solution.py:417
  122.3 0.7 copy.13
  (4 shorter events, 0.0 us)
Async XLA Ops:
  6.5 0.8 copy-start.5
  6.5 77.2 %all-gather.2.cloned.1.call-start = ((), (), s32[]{:S(2)}) async-start(), calls=%async_computation | async-start | bytes 1114112 | tf_op jit(solution)/shard_map/all_gather | solution.py:380
  6.5 0.8 copy-start.6
  7.3 0.7 copy-start.10
  8.0 1.0 copy-start.1
  8.9 1.0 copy-start.2
  9.9 1.0 copy-start.3
  10.9 0.9 copy-start.4
  11.9 0.8 copy-start.7
  12.6 0.8 copy-start.8
  13.4 0.7 copy-start.9
  83.7 1.2 copy-start
Sparse Core Ops, SparseCore 0:
  9.4 74.2 all-gather.1

commit v2 on v1

v2 whole, which is shorter than its diff:
```python
import jax
import jax.numpy as jnp
import numpy as np
from jax import lax
from jax.experimental import pallas as pl
from jax.experimental.pallas import tpu as pltpu
from jax.sharding import Mesh, PartitionSpec as P

F32 = jnp.float32
BF16 = jnp.bfloat16
CH = 8
VMEM = pl.BlockSpec(memory_space=pltpu.VMEM)


def split_hi_lo(table):
    high = table.astype(np.float32).astype(jnp.bfloat16)
    low = (table - high.astype(np.float64)).astype(np.float32).astype(jnp.bfloat16)
    return high, low


def tables(blocks, width):
    length = blocks * width
    f1 = np.arange(blocks)[:, None]
    a = np.exp(-2j * np.pi * ((np.arange(blocks)[None, :] * (4 * f1 + 1)) % (4 * blocks)) / (4 * blocks))
    t = np.exp(-2j * np.pi * (np.arange(width)[None, :] * (4 * f1 + 1)) / (4 * length))
    i = np.arange(width)
    b = np.exp(-2j * np.pi * ((i[:, None] * i[None, :]) % width) / width)
    a_high, a_low = split_hi_lo(np.concatenate([a.real, a.imag], 0))
    b_high, b_low = split_hi_lo(np.block([[b.real, b.imag], [-b.imag, b.real]]))
    c_high, c_low = split_hi_lo(np.block([[b.real, -b.imag], [b.imag, b.real]]))
    d_high, d_low = split_hi_lo(np.concatenate([a.real.T, a.imag.T], 1) / length)
    return (
        np.concatenate([a_high, a_low], 1),
        t.real.astype(np.float32),
        t.imag.astype(np.float32),
        np.concatenate([b_high, b_high, b_low], 0),
        np.concatenate([c_high, c_high, c_low], 0),
        np.concatenate([d_high, d_high, d_low], 1),
    )


def dot(left, right):
    return jnp.dot(left, right, preferred_element_type=F32)


def high_low(value):
    high = value.astype(BF16)
    return high, (value - high.astype(F32)).astype(BF16)


def send_all(chips, me, source, target, send_sem, recv_sem):
    def step(k, carry):
        peer = lax.rem(me + k, chips)
        pltpu.make_async_remote_copy(
            src_ref=source.at[peer],
            dst_ref=target.at[me],
            send_sem=send_sem,
            recv_sem=recv_sem,
            device_id={"z": peer // 2, "xh": lax.rem(peer, 2)},
        ).start()
        return carry

    lax.fori_loop(1, chips, step, 0)
    target[pl.ds(me, 1)] = source[pl.ds(me, 1)]


def wait_all(chips, ref, sem):
    part = ref.at[pl.ds(0, chips - 1)]
    pltpu.make_async_copy(part, part, sem).wait()


def spectrum(received, scratch, a_fwd, t_re, t_im, b_fwd):
    rows = scratch.shape[0]
    blocks = rows // CH
    scratch[...] = received[...].astype(F32).reshape(rows, -1)
    columns = [scratch[pl.ds(c, blocks, stride=CH), :].astype(BF16) for c in range(CH)]
    signal = jnp.concatenate(columns, axis=1)
    mixed = dot(a_fwd[...], jnp.concatenate([signal, signal], axis=0))
    width = t_re.shape[1]
    parts = []
    for c in range(CH):
        re = mixed[:blocks, c * width : (c + 1) * width]
        im = mixed[blocks:, c * width : (c + 1) * width]
        parts.append(
            jnp.concatenate(
                [re * t_re - im * t_im, re * t_im + im * t_re], axis=1
            )
        )
    high, low = high_low(jnp.concatenate(parts, axis=0))
    return dot(jnp.concatenate([high, low, high], axis=1), b_fwd[...])


def inverse(product, scratch, t_re, t_im, b_inv, a_inv):
    blocks, width = t_re.shape
    high, low = high_low(product)
    back = dot(jnp.concatenate([high, low, high], axis=1), b_inv[...])
    parts = []
    for c in range(CH):
        re = back[c * blocks : (c + 1) * blocks, :width]
        im = back[c * blocks : (c + 1) * blocks, width:]
        parts.append(
            jnp.concatenate(
                [re * t_re + im * t_im, im * t_re - re * t_im], axis=0
            )
        )
    high, low = high_low(jnp.concatenate(parts, axis=1))
    result = dot(a_inv[...], jnp.concatenate([high, low, high], axis=0))
    for c in range(CH):
        scratch[pl.ds(c, blocks, stride=CH), :] = result[:, c * width : (c + 1) * width]


def local_copy(source, target, sem):
    copy = pltpu.make_async_copy(source, target, sem)
    copy.start()
    return copy


def mixer_kernel(
    qkv_hbm, taps_hbm, filt_hbm, skip_hbm, weight_hbm,
    a_fwd_hbm, t_hbm, b_fwd_hbm, b_inv_hbm, a_inv_hbm,
    out,
    taps, filt, skip, a_fwd, t_both, b_fwd, b_inv, a_inv,
    h_own, h_pair, h_send, h_recv, x_all, u_send, u_recv, y_send, y_recv, scratch,
    weight, gated, g_all, parts, landed,
    load_sem, near_send, near_recv, far_send, far_recv,
    right_send, right_recv, left_send, left_recv, g_send, g_recv, part_send, part_recv,
):
    z, xh, core = lax.axis_index("z"), lax.axis_index("xh"), lax.axis_index("core")
    zs, xls = lax.axis_size("z"), lax.axis_size("xl")
    chips, groups = zs * 2, lax.axis_size("y") * xls
    me = z * 2 + xh
    owner_me = lax.axis_index("y") * xls + lax.axis_index("xl")
    slot = xh * 2 + core
    other = 1 - core
    rows = qkv_hbm.shape[1]
    half = chips * CH
    halo = 16
    mine = pl.ds(pl.multiple_of(core * half, half), half)
    theirs = pl.ds(pl.multiple_of(other * half, half), half)
    place = pl.ds(pl.multiple_of(halo + core * rows, 16), rows)
    everyone = 4 * groups
    my_index = slot * groups + owner_me

    filt_load = local_copy(filt_hbm, filt, load_sem.at[0])
    x_load = local_copy(qkv_hbm.at[:, :, mine], x_all.at[:, place, :], load_sem.at[1])
    weight_load = local_copy(weight_hbm, weight.at[z], load_sem.at[2])
    small = [
        local_copy(source, target, load_sem.at[3 + k])
        for k, (source, target) in enumerate(
            [
                (taps_hbm, taps),
                (skip_hbm, skip),
                (a_fwd_hbm, a_fwd),
                (t_hbm, t_both),
                (b_fwd_hbm, b_fwd),
                (b_inv_hbm, b_inv),
                (a_inv_hbm, a_inv),
            ]
        )
    ]

    barrier = pltpu.get_barrier_semaphore()
    step_to = lax.rem(me + jnp.where(core == 1, 1, chips - 1), chips)
    pl.semaphore_signal(
        barrier, inc=1, device_id={"z": step_to // 2, "xh": lax.rem(step_to, 2), "core": other}
    )

    def place_of(index):
        which, owner = index // groups, lax.rem(index, groups)
        return {
            "xh": which // 2,
            "core": lax.rem(which, 2),
            "y": owner // xls,
            "xl": lax.rem(owner, xls),
        }

    def greet_ctx(k, carry):
        peer = lax.rem(me + k, chips)
        pl.semaphore_signal(
            barrier, inc=1, device_id={"z": peer // 2, "xh": lax.rem(peer, 2)}
        )
        return carry

    def greet_plane(k, carry):
        pl.semaphore_signal(barrier, inc=1, device_id=place_of(lax.rem(my_index + k, everyone)))
        return carry

    lax.fori_loop(1, chips, greet_ctx, 0)
    lax.fori_loop(1, everyone, greet_plane, 0)

    filt_load.wait()
    h_own[...] = filt[...].T.reshape(2, chips, CH, rows)
    pl.semaphore_wait(barrier, 1 + chips - 1 + everyone - 1)

    my_rows = pl.ds(pl.multiple_of(core * CH, CH), CH)
    h_copy = pltpu.make_async_remote_copy(
        src_ref=h_own.at[other],
        dst_ref=h_pair.at[:, my_rows, :],
        send_sem=near_send.at[0],
        recv_sem=near_recv.at[0],
        device_id={"core": other},
    )
    h_copy.start()
    x_copy = pltpu.make_async_remote_copy(
        src_ref=qkv_hbm.at[:, :, theirs],
        dst_ref=x_all.at[:, place, :],
        send_sem=near_send.at[1],
        recv_sem=near_recv.at[1],
        device_id={"core": other},
    )
    x_copy.start()

    after = lax.rem(me + 1, chips)

    def halo_copy(target):
        return pltpu.make_async_remote_copy(
            src_ref=qkv_hbm.at[:, pl.ds(rows - halo, halo), pl.ds(target * half, half)],
            dst_ref=x_all.at[:, pl.ds(0, halo), :],
            send_sem=near_send.at[2 + target],
            recv_sem=near_recv.at[2],
            device_id={"z": after // 2, "xh": lax.rem(after, 2), "core": target},
        )

    @pl.when(core == 1)
    def _():
        halo_copy(0).start()
        halo_copy(1).start()

    right_steps = zs // 2
    left_steps = zs - 1 - right_steps

    def right_copy(step):
        block = lax.rem(z + zs - step, zs)
        return pltpu.make_async_remote_copy(
            src_ref=weight.at[block],
            dst_ref=weight.at[block],
            send_sem=right_send.at[step],
            recv_sem=right_recv.at[step],
            device_id={"z": lax.rem(z + 1, zs)},
        )

    def left_copy(step):
        block = lax.rem(z + step, zs)
        return pltpu.make_async_remote_copy(
            src_ref=weight.at[block],
            dst_ref=weight.at[block],
            send_sem=left_send.at[step],
            recv_sem=left_recv.at[step],
            device_id={"z": lax.rem(z + zs - 1, zs)},
        )

    def landing(step, shift, sem):
        block = weight.at[lax.rem(z + shift, zs)]
        pltpu.make_async_copy(block, block, sem.at[step]).wait()

    def ring(step):
        if step == 0:
            weight_load.wait()
        if 0 < step <= right_steps:
            landing(step - 1, zs - step, right_recv)
        if 0 < step <= left_steps:
            landing(step - 1, step, left_recv)
        if step < right_steps:
            right_copy(step).start()
        if step < left_steps:
            left_copy(step).start()

    ring(0)
    h_pair[:, my_rows, :] = h_own[pl.ds(core, 1)].reshape(chips, CH, rows)
    h_copy.wait_recv()
    h_send[...] = h_pair[...].astype(BF16)
    send_all(chips, me, h_send, h_recv, far_send.at[0], far_recv.at[0])

    x_load.wait()
    small[0].wait()
    x_copy.wait_recv()
    halo_copy(0).wait_recv()
    features = []
    for s in range(3):
        x = x_all[s].astype(F32)
        first = jnp.where(me == 0, 0.0, x[:halo])
        x = jnp.concatenate([first, x[halo:]], axis=0)
        total = taps[s, 0:1, mine] * x[halo:]
        for back in range(1, taps.shape[1]):
            total = total + taps[s, back : back + 1, mine] * x[halo - back : halo - back + 2 * rows]
        features.append(total)
    query, mixed_in = features[0], features[1] * features[2]
    flipped = mixed_in.T.reshape(chips, CH, 2 * rows)
    u_send[...] = jnp.concatenate([flipped[:, :, :rows], flipped[:, :, rows:]], axis=1).astype(BF16)
    send_all(chips, me, u_send, u_recv, far_send.at[1], far_recv.at[1])
    ring(1)

    for load in small[1:]:
        load.wait()
    wait_all(chips, h_recv, far_recv.at[0])
    ring(2)
    t_re, t_im = t_both[0], t_both[1]
    h_freq = spectrum(h_recv, scratch, a_fwd, t_re, t_im, b_fwd)
    ring(3)
    wait_all(chips, u_recv, far_recv.at[1])
    ring(4)
    u_freq = spectrum(u_recv, scratch, a_fwd, t_re, t_im, b_fwd)
    ring(5)
    width = t_re.shape[1]
    h_re, h_im = h_freq[:, :width], h_freq[:, width:]
    u_re, u_im = u_freq[:, :width], u_freq[:, width:]
    product = jnp.concatenate([h_re * u_re - h_im * u_im, h_re * u_im + h_im * u_re], axis=1)
    inverse(product, scratch, t_re, t_im, b_inv, a_inv)
    y_send[...] = scratch[...].reshape(y_send.shape).astype(BF16)
    send_all(chips, me, y_send, y_recv, far_send.at[2], far_recv.at[2])
    ring(6)
    ring(7)
    wait_all(chips, y_recv, far_recv.at[2])
    for step in range(8, right_steps + 1):
        ring(step)
    back = y_recv[...].astype(F32)
    convolved = jnp.concatenate(
        [back[:, CH * b : CH * (b + 1), :].reshape(half, rows).T for b in range(2)], axis=0
    )
    gated[...] = (query * (convolved + skip[:, mine] * mixed_in)).astype(BF16)

    copies = []
    for far in range(2):
        for cross in range(2):
            if far == 0 and cross == 0:
                continue
            index = far * 2 + cross - 1
            copies.append(
                pltpu.make_async_remote_copy(
                    src_ref=gated,
                    dst_ref=g_all.at[xh, :, mine],
                    send_sem=g_send.at[index],
                    recv_sem=g_recv.at[index],
                    device_id={"xh": 1 - xh if far else xh, "core": other if cross else core},
                )
            )
    for copy in copies:
        copy.start()
    tokens = 2 * rows
    g_all[pl.ds(xh, 1), :, mine] = gated[...].reshape(1, tokens, half)
    per_owner = zs // groups
    columns = weight.shape[1]
    wide = per_owner * columns

    def send(which_x, b, owner):
        pltpu.make_async_remote_copy(
            src_ref=parts.at[which_x, b, owner],
            dst_ref=landed.at[slot, owner_me],
            send_sem=part_send,
            recv_sem=part_recv.at[slot, owner_me],
            device_id={"xh": which_x, "core": b, "y": owner // xls, "xl": lax.rem(owner, xls)},
        ).start()

    def compute(which_x, owner):
        block = weight[pl.ds(owner * per_owner, per_owner)].reshape(wide, 2 * half)
        left = g_all[pl.ds(which_x, 1)].reshape(tokens, 2 * half)
        product = lax.dot_general(
            left, block, (((1,), (1,)), ((), ())), preferred_element_type=F32
        ).astype(BF16)
        for b in range(2):
            parts[pl.ds(which_x, 1), b, pl.ds(owner, 1)] = product[
                b * rows : (b + 1) * rows
            ].reshape(1, 1, rows, wide)

    copies[0].wait_recv()

    def own_step(k, carry):
        owner = lax.rem(owner_me + k, groups)
        compute(xh, owner)
        for b in range(2):
            send(xh, b, owner)
        return carry

    lax.fori_loop(1, groups, own_step, 0)
    compute(xh, owner_me)
    send(xh, other, owner_me)
    landed[pl.ds(slot, 1), pl.ds(owner_me, 1)] = parts[
        pl.ds(xh, 1), pl.ds(core, 1), pl.ds(owner_me, 1)
    ].reshape(1, 1, rows, wide)
    copies[1].wait_recv()
    copies[2].wait_recv()

    def far_step(k, carry):
        owner = lax.rem(owner_me + k, groups)
        compute(1 - xh, owner)
        for b in range(2):
            send(1 - xh, b, owner)
        return carry

    lax.fori_loop(0, groups, far_step, 0)

    def arrived(k, carry):
        index = lax.rem(my_index + k, everyone)
        which, owner = index // groups, lax.rem(index, groups)
        block = landed.at[which, owner]
        pltpu.make_async_copy(block, block, part_recv.at[which, owner]).wait()
        return carry

    lax.fori_loop(1, everyone, arrived, 0)
    sums = []
    for s in range(4):
        total = landed[s, 0].astype(F32)
        for owner in range(1, groups):
            total = total + landed[s, owner].astype(F32)
        sums.append(total)
    for part in range(per_owner):
        pieces = [total[:, part * columns : (part + 1) * columns] for total in sums]
        out[:, part * 4 * columns : (part + 1) * 4 * columns] = jnp.concatenate(
            pieces, axis=1
        ).astype(out.dtype)

    h_copy.wait_send()
    x_copy.wait_send()

    @pl.when(core == 1)
    def _():
        halo_copy(0).wait_send()
        halo_copy(1).wait_send()

    for step in range(right_steps):
        right_copy(step).wait_send()
    for step in range(left_steps):
        left_copy(step).wait_send()
    wait_all(chips, h_send, far_send.at[0])
    wait_all(chips, u_send, far_send.at[1])
    wait_all(chips, y_send, far_send.at[2])
    for copy in copies:
        copy.wait_send()
    for sent in (parts.at[0, 0, pl.ds(0, groups - 1)], parts.at[0, 1], parts.at[1]):
        pltpu.make_async_copy(sent, sent, part_send).wait()


def body(qkv_in, short_taps, long_filter, skip_gain, out_weight):
    rows, _, channels = qkv_in.shape
    half = channels // 2
    zs = lax.axis_size("z")
    chips = zs * 2
    groups = lax.axis_size("y") * lax.axis_size("xl")
    blocks = 2 * chips
    columns = out_weight.shape[1]
    wide = zs // groups * columns
    a_fwd, t_re, t_im, b_fwd, b_inv, a_inv = tables(blocks, rows)
    lookup = [jnp.asarray(table) for table in (a_fwd, np.stack([t_re, t_im]), b_fwd, b_inv, a_inv)]
    exchange = (chips, 2 * CH, rows)
    dma = pltpu.SemaphoreType.DMA
    return pl.pallas_call(
        mixer_kernel,
        out_shape=jax.ShapeDtypeStruct((rows, channels), BF16),
        in_specs=[pl.BlockSpec(memory_space=pl.ANY)] * 10,
        out_specs=VMEM,
        scratch_shapes=[
            pltpu.VMEM(short_taps.shape, F32),
            pltpu.VMEM((rows, channels), F32),
            pltpu.VMEM((1, channels), F32),
            *[pltpu.VMEM(table.shape, table.dtype) for table in lookup],
            pltpu.VMEM((2, chips, CH, rows), F32),
            pltpu.VMEM(exchange, F32),
            pltpu.VMEM(exchange, BF16),
            pltpu.VMEM(exchange, BF16),
            pltpu.VMEM((3, 16 + 2 * rows, half), BF16),
            pltpu.VMEM(exchange, BF16),
            pltpu.VMEM(exchange, BF16),
            pltpu.VMEM(exchange, BF16),
            pltpu.VMEM(exchange, BF16),
            pltpu.VMEM((blocks * CH, rows), F32),
            pltpu.VMEM((zs, columns, channels), BF16),
            pltpu.VMEM((2 * rows, half), BF16),
            pltpu.VMEM((2, 2 * rows, channels), BF16),
            pltpu.VMEM((2, 2, groups, rows, wide), BF16),
            pltpu.VMEM((4, groups, rows, wide), BF16),
            dma((10,)),
            dma((4,)),
            dma((3,)),
            dma((3,)),
            dma((3,)),
            dma((zs,)),
            dma((zs,)),
            dma((zs,)),
            dma((zs,)),
            dma((3,)),
            dma((3,)),
            dma,
            dma((4, groups)),
        ],
        compiler_params=pltpu.CompilerParams(
            collective_id=0, has_side_effects=True, vmem_limit_bytes=48 * 2**20
        ),
        name="mixer",
    )(
        qkv_in.transpose(1, 0, 2),
        short_taps,
        long_filter,
        skip_gain[None, :],
        out_weight.T,
        *lookup,
    )


def solution(mesh):
    sizes = dict(mesh.shape)
    split = Mesh(
        mesh.devices.reshape(sizes["ctx"] // 4, 2, 2, sizes["tp"] // 2, 2),
        ("z", "xh", "core", "y", "xl"),
    )
    ctx, tp = ("z", "xh", "core"), ("y", "xl")
    return jax.shard_map(
        body,
        mesh=split,
        in_specs=(P(ctx, None, tp), P(None, None, tp), P(ctx, tp), P(tp), P(tp, ctx)),
        out_specs=P(ctx, tp),
        check_vma=False,
    )
```

time: 130 us -> 92 us (0.71)
  waiting for transfers between devices: 20.2 us -> 0 us
  between operations: 13.4 us -> 0.02 us
  Pallas kernels: 87.4 us -> 82.1 us
    all_gather x1 -> x0, waiting for transfers between devices: 19.5 us -> none  [body(): weight = lax.all_gather(out_weight.T, 'z', axis=0, tiled=True)]
    pallas_call x2 -> x1, Pallas kernels: 87.4 us -> 82.1 us  [body(): pl.pallas_call(mixer_kernel, out_shape=jax.ShapeDtypeStruct((rows, channe...]
    unnamed x23 -> x21, local copies, waits for them, and re-layouts: 8.76 us -> 9.24 us
  transfers between devices with their start and end apart: 1 -> 0, of which waited for: 1 -> 0; matrix products, arithmetic and copies ran while one was open for 0% -> 0% of each run, Pallas kernels for 39% -> 0%
where the time goes in v2:
time: 92 us; the launch traced here: 91.4 us
  Pallas kernels  82.1 us (89%)
  local copies, waits for them, and re-layouts  9.24 us (10%)
    pallas_call x1, Pallas kernels, body(): pl.pallas_call(mixer_kernel, out_shape=jax.ShapeDtypeStruct((rows, channe...  82.1 us
    unnamed x21, local copies, waits for them, and re-layouts  9.24 us

profile of v2, /device:TPU:1, one launch (start us, length us, event | category | flops | bytes accessed | tf_op | source)
XLA Modules:
  0.0 91.4 jit_solution(15175258076555110014)
XLA Ops:
  0.0 0.0 copy-start.9
  0.0 0.7 copy-done.9
  0.7 0.0 copy-start
  0.7 1.0 %copy-done = bf16[128,3,512]{2,0,1:T(8,128)(2,1)S(1)} copy-done((bf16[128,3,512]{2,0,1:T(8,128)(2,1)S(1)}, bf16[128,3,512]{2,0,1:T(8,128)(2,1)}, u32[]{:S(2)}) %copy-start) | copy-done | bytes 393240
  1.7 0.0 copy-start.1
  1.7 1.0 %copy-done.1 = bf16[768,256]{1,0:T(8,128)(2,1)S(1)} copy-done((bf16[768,256]{1,0:T(8,128)(2,1)S(1)}, bf16[768,256]{1,0:T(8,128)(2,1)}, u32[]{:S(2)}) %copy-start.1) | copy-done | bytes 393240
  2.7 0.0 copy-start.2
  2.7 1.0 %copy-done.2 = bf16[768,256]{1,0:T(8,128)(2,1)S(1)} copy-done((bf16[768,256]{1,0:T(8,128)(2,1)S(1)}, bf16[768,256]{1,0:T(8,128)(2,1)}, u32[]{:S(2)}) %copy-start.2) | copy-done | bytes 393240
  3.7 0.0 copy-start.3
  3.7 0.9 %copy-done.3 = f32[128,512]{1,0:T(8,128)S(1)} copy-done((f32[128,512]{1,0:T(8,128)S(1)}, f32[128,512]{1,0:T(8,128)}, u32[]{:S(2)}) %copy-start.3) | copy-done | bytes 262168
  4.6 0.0 copy-start.4
  4.6 0.8 copy-done.4
  5.5 0.0 copy-start.5
  5.5 0.8 copy-done.5
  6.3 0.0 copy-start.6
  6.3 0.8 copy-done.6
  7.1 0.0 copy-start.7
  7.1 0.8 copy-done.7
  7.9 0.0 copy-start.8
  7.9 0.7 copy-done.8
  8.6 82.1 %mixer.1 = bf16[128,512]{1,0:T(8,128)(2,1)S(1)} custom-call(bf16[3,128,512]{2,1,0:T(8,128)(2,1)S(1)} %bitcast.3, f32[3,3,512]{2,1,0:T(4,128)S(1)} %copy-done.8, f32[128,512]{1,0:T(8,128)S(1)} %copy-done.3, f32[1,512]{1,0:T(1,128)S(1)} %bitcast.5, bf16[64,512]{1,0:T(8,128)(2,1)S(1)} %bitcast.4, bf16[128,128]{1,0:T(8,128)(2,1)S(1)} %copy-done.7, ...), custom_call_target="tpu_custom_call" | custom-call | tf_op jit(solution)/shard_map/mixer/pallas_call | solution.py:446
  90.7 0.7 copy.12
Async XLA Ops:
  0.0 0.7 copy-start.9
  0.7 1.0 %copy-start = (bf16[128,3,512]{2,0,1:T(8,128)(2,1)S(1)}, bf16[128,3,512]{2,0,1:T(8,128)(2,1)}, u32[]{:S(2)}) copy-start(bf16[128,3,512]{2,0,1:T(8,128)(2,1)} %param.10) | copy-start | bytes 1179652
  1.7 1.0 %copy-start.1 = (bf16[768,256]{1,0:T(8,128)(2,1)S(1)}, bf16[768,256]{1,0:T(8,128)(2,1)}, u32[]{:S(2)}) copy-start(bf16[768,256]{1,0:T(8,128)(2,1)} %constant.13.clone.b_inv_hbm) | copy-start | bytes 1179652
  2.7 1.0 %copy-start.2 = (bf16[768,256]{1,0:T(8,128)(2,1)S(1)}, bf16[768,256]{1,0:T(8,128)(2,1)}, u32[]{:S(2)}) copy-start(bf16[768,256]{1,0:T(8,128)(2,1)} %constant.12.clone.b_fwd_hbm) | copy-start | bytes 1179652
  3.7 0.9 %copy-start.3 = (f32[128,512]{1,0:T(8,128)S(1)}, f32[128,512]{1,0:T(8,128)}, u32[]{:S(2)}) copy-start(f32[128,512]{1,0:T(8,128)} %filt_hbm.1) | copy-start | bytes 786436
  4.6 0.8 copy-start.4
  5.5 0.8 copy-start.5
  6.3 0.8 copy-start.6
  7.1 0.8 copy-start.7
  7.9 0.7 copy-start.8

commit v3 on v2

--- a/solution.py
+++ b/solution.py
@@ -12,12 +12,6 @@
 VMEM = pl.BlockSpec(memory_space=pltpu.VMEM)
 
 
-def split_hi_lo(table):
-    high = table.astype(np.float32).astype(jnp.bfloat16)
-    low = (table - high.astype(np.float64)).astype(np.float32).astype(jnp.bfloat16)
-    return high, low
-
-
 def tables(blocks, width):
     length = blocks * width
     f1 = np.arange(blocks)[:, None]
@@ -25,18 +19,13 @@
     t = np.exp(-2j * np.pi * (np.arange(width)[None, :] * (4 * f1 + 1)) / (4 * length))
     i = np.arange(width)
     b = np.exp(-2j * np.pi * ((i[:, None] * i[None, :]) % width) / width)
-    a_high, a_low = split_hi_lo(np.concatenate([a.real, a.imag], 0))
-    b_high, b_low = split_hi_lo(np.block([[b.real, b.imag], [-b.imag, b.real]]))
-    c_high, c_low = split_hi_lo(np.block([[b.real, -b.imag], [b.imag, b.real]]))
-    d_high, d_low = split_hi_lo(np.concatenate([a.real.T, a.imag.T], 1) / length)
-    return (
-        np.concatenate([a_high, a_low], 1),
-        t.real.astype(np.float32),
-        t.imag.astype(np.float32),
-        np.concatenate([b_high, b_high, b_low], 0),
-        np.concatenate([c_high, c_high, c_low], 0),
-        np.concatenate([d_high, d_high, d_low], 1),
-    )
+    found = (
+        np.concatenate([a.real, a.imag], 0),
+        np.stack([t.real, t.imag]),
+        np.block([[b.real, b.imag], [-b.imag, b.real]]),
+        np.concatenate([a.real.T, a.imag.T], 1) / length,
+    )
+    return [jnp.asarray(table.astype(np.float32)) for table in found]
 
 
 def dot(left, right):
@@ -69,7 +58,7 @@
     pltpu.make_async_copy(part, part, sem).wait()
 
 
-def spectrum(received, scratch, a_fwd, t_re, t_im, b_fwd):
+def spectrum(received, scratch, a_fwd, t_re, t_im, b_dft):
     rows = scratch.shape[0]
     blocks = rows // CH
     scratch[...] = received[...].astype(F32).reshape(rows, -1)
@@ -87,17 +76,17 @@
             )
         )
     high, low = high_low(jnp.concatenate(parts, axis=0))
-    return dot(jnp.concatenate([high, low, high], axis=1), b_fwd[...])
-
-
-def inverse(product, scratch, t_re, t_im, b_inv, a_inv):
+    return dot(jnp.concatenate([high, low, high], axis=1), b_dft[...])
+
+
+def inverse(product, scratch, t_re, t_im, b_dft, a_inv):
     blocks, width = t_re.shape
     high, low = high_low(product)
-    back = dot(jnp.concatenate([high, low, high], axis=1), b_inv[...])
+    back = dot(jnp.concatenate([high, low, high], axis=1), b_dft[...])
     parts = []
     for c in range(CH):
-        re = back[c * blocks : (c + 1) * blocks, :width]
-        im = back[c * blocks : (c + 1) * blocks, width:]
+        im = back[c * blocks : (c + 1) * blocks, :width]
+        re = back[c * blocks : (c + 1) * blocks, width:]
         parts.append(
             jnp.concatenate(
                 [re * t_re + im * t_im, im * t_re - re * t_im], axis=0
@@ -117,9 +106,9 @@
 
 def mixer_kernel(
     qkv_hbm, taps_hbm, filt_hbm, skip_hbm, weight_hbm,
-    a_fwd_hbm, t_hbm, b_fwd_hbm, b_inv_hbm, a_inv_hbm,
+    a_fwd_hbm, t_hbm, b_dft_hbm, a_inv_hbm,
     out,
-    taps, filt, skip, a_fwd, t_both, b_fwd, b_inv, a_inv,
+    taps, filt, skip, a_table, t_both, b_table, a_back, a_fwd, b_dft, a_inv,
     h_own, h_pair, h_send, h_recv, x_all, u_send, u_recv, y_send, y_recv, scratch,
     weight, gated, g_all, parts, landed,
     load_sem, near_send, near_recv, far_send, far_recv,
@@ -150,11 +139,10 @@
             [
                 (taps_hbm, taps),
                 (skip_hbm, skip),
-                (a_fwd_hbm, a_fwd),
+                (a_fwd_hbm, a_table),
                 (t_hbm, t_both),
-                (b_fwd_hbm, b_fwd),
-                (b_inv_hbm, b_inv),
-                (a_inv_hbm, a_inv),
+                (b_dft_hbm, b_table),
+                (a_inv_hbm, a_back),
             ]
         )
     ]
@@ -292,20 +280,25 @@
 
     for load in small[1:]:
         load.wait()
+    a_fwd[...] = jnp.concatenate(high_low(a_table[...]), axis=1)
+    high, low = high_low(b_table[...])
+    b_dft[...] = jnp.concatenate([high, high, low], axis=0)
+    high, low = high_low(a_back[...])
+    a_inv[...] = jnp.concatenate([high, high, low], axis=1)
     wait_all(chips, h_recv, far_recv.at[0])
     ring(2)
     t_re, t_im = t_both[0], t_both[1]
-    h_freq = spectrum(h_recv, scratch, a_fwd, t_re, t_im, b_fwd)
+    h_freq = spectrum(h_recv, scratch, a_fwd, t_re, t_im, b_dft)
     ring(3)
     wait_all(chips, u_recv, far_recv.at[1])
     ring(4)
-    u_freq = spectrum(u_recv, scratch, a_fwd, t_re, t_im, b_fwd)
+    u_freq = spectrum(u_recv, scratch, a_fwd, t_re, t_im, b_dft)
     ring(5)
     width = t_re.shape[1]
     h_re, h_im = h_freq[:, :width], h_freq[:, width:]
     u_re, u_im = u_freq[:, :width], u_freq[:, width:]
-    product = jnp.concatenate([h_re * u_re - h_im * u_im, h_re * u_im + h_im * u_re], axis=1)
-    inverse(product, scratch, t_re, t_im, b_inv, a_inv)
+    product = jnp.concatenate([h_re * u_im + h_im * u_re, h_re * u_re - h_im * u_im], axis=1)
+    inverse(product, scratch, t_re, t_im, b_dft, a_inv)
     y_send[...] = scratch[...].reshape(y_send.shape).astype(BF16)
     send_all(chips, me, y_send, y_recv, far_send.at[2], far_recv.at[2])
     ring(6)
@@ -439,20 +432,22 @@
     blocks = 2 * chips
     columns = out_weight.shape[1]
     wide = zs // groups * columns
-    a_fwd, t_re, t_im, b_fwd, b_inv, a_inv = tables(blocks, rows)
-    lookup = [jnp.asarray(table) for table in (a_fwd, np.stack([t_re, t_im]), b_fwd, b_inv, a_inv)]
+    lookup = tables(blocks, rows)
     exchange = (chips, 2 * CH, rows)
     dma = pltpu.SemaphoreType.DMA
     return pl.pallas_call(
         mixer_kernel,
         out_shape=jax.ShapeDtypeStruct((rows, channels), BF16),
-        in_specs=[pl.BlockSpec(memory_space=pl.ANY)] * 10,
+        in_specs=[pl.BlockSpec(memory_space=pl.ANY)] * 9,
         out_specs=VMEM,
         scratch_shapes=[
             pltpu.VMEM(short_taps.shape, F32),
             pltpu.VMEM((rows, channels), F32),
             pltpu.VMEM((1, channels), F32),
             *[pltpu.VMEM(table.shape, table.dtype) for table in lookup],
+            pltpu.VMEM((2 * blocks, 2 * blocks), BF16),
+            pltpu.VMEM((6 * rows, 2 * rows), BF16),
+            pltpu.VMEM((blocks, 6 * blocks), BF16),
             pltpu.VMEM((2, chips, CH, rows), F32),
             pltpu.VMEM(exchange, F32),
             pltpu.VMEM(exchange, BF16),
@@ -468,7 +463,7 @@
             pltpu.VMEM((2, 2 * rows, channels), BF16),
             pltpu.VMEM((2, 2, groups, rows, wide), BF16),
             pltpu.VMEM((4, groups, rows, wide), BF16),
-            dma((10,)),
+            dma((9,)),
             dma((4,)),
             dma((3,)),
             dma((3,)),
@@ -483,7 +478,7 @@
             dma((4, groups)),
         ],
         compiler_params=pltpu.CompilerParams(
-            collective_id=0, has_side_effects=True, vmem_limit_bytes=48 * 2**20
+            collective_id=0, has_side_effects=True, vmem_limit_bytes=60 * 2**20
         ),
         name="mixer",
     )(

time: 92 us -> 85 us (0.924)
  local copies, waits for them, and re-layouts: 9.24 us -> 1.57 us
  Pallas kernels: 82.1 us -> 83.3 us
    unnamed x21 -> x1, local copies, waits for them, and re-layouts: 9.24 us -> 1.57 us
    pallas_call x1, Pallas kernels: 82.1 us -> 83.3 us  [body(): pl.pallas_call(mixer_kernel, out_shape=jax.ShapeDtypeStruct((rows, channe...]
where the time goes in v3:
time: 85 us; the launch traced here: 84.9 us
  Pallas kernels  83.3 us (98%)
  local copies, waits for them, and re-layouts  1.57 us (2%)
    pallas_call x1, Pallas kernels, body(): pl.pallas_call(mixer_kernel, out_shape=jax.ShapeDtypeStruct((rows, channe...  83.3 us

profile of v3, /device:TPU:1, one launch (start us, length us, event | category | flops | bytes accessed | tf_op | source)
XLA Modules:
  0.0 84.9 jit_solution(2441420115094440165)
XLA Ops:
  0.0 83.3 %mixer.1 = bf16[128,512]{1,0:T(8,128)(2,1)} custom-call(bf16[3,128,512]{2,1,0:T(8,128)(2,1)} %bitcast.3, f32[3,3,512]{2,1,0:T(4,128)} %taps_hbm.1, f32[128,512]{1,0:T(8,128)} %filt_hbm.1, f32[1,512]{1,0:T(1,128)} %bitcast.5, bf16[64,512]{1,0:T(8,128)(2,1)} %bitcast.4, f32[128,64]{1,0:T(8,128)} %constant.8.clone.a_fwd_hbm, ...), custom_call_target="tpu_custom_call" | custom-call | tf_op jit(solution)/shard_map/mixer/pallas_call | solution.py:438
  83.3 1.6 %copy.11 = bf16[128,512]{1,0:T(8,128)(2,1)} copy(bf16[128,512]{1,0:T(8,128)(2,1)} %mixer.1) | data formatting | bytes 262144

commit v4 on v3

--- a/solution.py
+++ b/solution.py
@@ -37,19 +37,25 @@
     return high, (value - high.astype(F32)).astype(BF16)
 
 
-def send_all(chips, me, source, target, send_sem, recv_sem):
+def send_all(z, xh, source, target, send_sem, recv_sem):
+    zs = lax.axis_size("z")
+    me = z * 2 + xh
+
     def step(k, carry):
-        peer = lax.rem(me + k, chips)
+        turn = k // 2
+        ahead = zs // 2 + jnp.where(lax.rem(turn, 2) == 1, -((turn + 1) // 2), turn // 2)
+        to_z = lax.rem(z + ahead, zs)
+        to_x = jnp.where(lax.rem(k, 2) == 0, 1 - xh, xh)
         pltpu.make_async_remote_copy(
-            src_ref=source.at[peer],
+            src_ref=source.at[to_z * 2 + to_x],
             dst_ref=target.at[me],
             send_sem=send_sem,
             recv_sem=recv_sem,
-            device_id={"z": peer // 2, "xh": lax.rem(peer, 2)},
+            device_id={"z": to_z, "xh": to_x},
         ).start()
         return carry
 
-    lax.fori_loop(1, chips, step, 0)
+    lax.fori_loop(0, 2 * zs - 1, step, 0)
     target[pl.ds(me, 1)] = source[pl.ds(me, 1)]
 
 
@@ -115,10 +121,11 @@
     right_send, right_recv, left_send, left_recv, g_send, g_recv, part_send, part_recv,
 ):
     z, xh, core = lax.axis_index("z"), lax.axis_index("xh"), lax.axis_index("core")
-    zs, xls = lax.axis_size("z"), lax.axis_size("xl")
-    chips, groups = zs * 2, lax.axis_size("y") * xls
+    y, xl = lax.axis_index("y"), lax.axis_index("xl")
+    zs, ys = lax.axis_size("z"), lax.axis_size("y")
+    chips = zs * 2
+    per_owner = zs // (2 * ys)
     me = z * 2 + xh
-    owner_me = lax.axis_index("y") * xls + lax.axis_index("xl")
     slot = xh * 2 + core
     other = 1 - core
     rows = qkv_hbm.shape[1]
@@ -127,12 +134,27 @@
     mine = pl.ds(pl.multiple_of(core * half, half), half)
     theirs = pl.ds(pl.multiple_of(other * half, half), half)
     place = pl.ds(pl.multiple_of(halo + core * rows, 16), rows)
-    everyone = 4 * groups
-    my_index = slot * groups + owner_me
+    everyone = 4 * ys
+    my_index = slot * ys + y
+    x = xh * 2 + xl
+    up, down = lax.rem(x + 1, 4), lax.rem(x + 3, 4)
+    up_x = {"xh": up // 2, "xl": lax.rem(up, 2)}
+    down_x = {"xh": down // 2, "xl": lax.rem(down, 2)}
+
+    def on(block):
+        return lax.rem(block // per_owner, 2) == xl
+
+    def spot(block):
+        return block // (2 * per_owner) * per_owner + lax.rem(block, per_owner)
 
     filt_load = local_copy(filt_hbm, filt, load_sem.at[0])
     x_load = local_copy(qkv_hbm.at[:, :, mine], x_all.at[:, place, :], load_sem.at[1])
-    weight_load = local_copy(weight_hbm, weight.at[z], load_sem.at[2])
+    weight_load = pltpu.make_async_copy(weight_hbm, weight.at[spot(z), xl], load_sem.at[2])
+
+    @pl.when(on(z))
+    def _():
+        weight_load.start()
+
     small = [
         local_copy(source, target, load_sem.at[3 + k])
         for k, (source, target) in enumerate(
@@ -153,14 +175,12 @@
         barrier, inc=1, device_id={"z": step_to // 2, "xh": lax.rem(step_to, 2), "core": other}
     )
 
+    pl.semaphore_signal(barrier, inc=1, device_id=up_x)
+    pl.semaphore_signal(barrier, inc=1, device_id=down_x)
+
     def place_of(index):
-        which, owner = index // groups, lax.rem(index, groups)
-        return {
-            "xh": which // 2,
-            "core": lax.rem(which, 2),
-            "y": owner // xls,
-            "xl": lax.rem(owner, xls),
-        }
+        which = index // ys
+        return {"xh": which // 2, "core": lax.rem(which, 2), "y": lax.rem(index, ys)}
 
     def greet_ctx(k, carry):
         peer = lax.rem(me + k, chips)
@@ -178,7 +198,7 @@
 
     filt_load.wait()
     h_own[...] = filt[...].T.reshape(2, chips, CH, rows)
-    pl.semaphore_wait(barrier, 1 + chips - 1 + everyone - 1)
+    pl.semaphore_wait(barrier, 3 + chips - 1 + everyone - 1)
 
     my_rows = pl.ds(pl.multiple_of(core * CH, CH), CH)
     h_copy = pltpu.make_async_remote_copy(
@@ -214,50 +234,75 @@
         halo_copy(0).start()
         halo_copy(1).start()
 
+    swap = pltpu.make_async_remote_copy(
+        src_ref=weight_hbm,
+        dst_ref=weight.at[spot(z), xl],
+        send_sem=near_send.at[4],
+        recv_sem=near_recv.at[3],
+        device_id={"xl": 1 - xl},
+    )
+
+    @pl.when(jnp.logical_not(on(z)))
+    def _():
+        swap.start()
+
     right_steps = zs // 2
     left_steps = zs - 1 - right_steps
 
+    def pass_on(block, step, send_sem, recv_sem, ahead):
+        return pltpu.make_async_remote_copy(
+            src_ref=weight.at[spot(block)],
+            dst_ref=weight.at[spot(block)],
+            send_sem=send_sem.at[step],
+            recv_sem=recv_sem.at[step],
+            device_id={"z": lax.rem(z + ahead, zs)},
+        )
+
     def right_copy(step):
-        block = lax.rem(z + zs - step, zs)
-        return pltpu.make_async_remote_copy(
-            src_ref=weight.at[block],
-            dst_ref=weight.at[block],
-            send_sem=right_send.at[step],
-            recv_sem=right_recv.at[step],
-            device_id={"z": lax.rem(z + 1, zs)},
-        )
+        return pass_on(lax.rem(z + zs - step, zs), step, right_send, right_recv, 1)
 
     def left_copy(step):
-        block = lax.rem(z + step, zs)
-        return pltpu.make_async_remote_copy(
-            src_ref=weight.at[block],
-            dst_ref=weight.at[block],
-            send_sem=left_send.at[step],
-            recv_sem=left_recv.at[step],
-            device_id={"z": lax.rem(z + zs - 1, zs)},
-        )
+        return pass_on(lax.rem(z + step, zs), step, left_send, left_recv, zs - 1)
 
     def landing(step, shift, sem):
-        block = weight.at[lax.rem(z + shift, zs)]
-        pltpu.make_async_copy(block, block, sem.at[step]).wait()
+        block = lax.rem(z + shift, zs)
+
+        @pl.when(on(block))
+        def _():
+            landed_at = weight.at[spot(block)]
+            pltpu.make_async_copy(landed_at, landed_at, sem.at[step]).wait()
 
     def ring(step):
+        if step > right_steps:
+            return
         if step == 0:
-            weight_load.wait()
+
+            @pl.when(on(z))
+            def _():
+                weight_load.wait()
+                swap.wait_recv()
+
         if 0 < step <= right_steps:
             landing(step - 1, zs - step, right_recv)
         if 0 < step <= left_steps:
             landing(step - 1, step, left_recv)
         if step < right_steps:
-            right_copy(step).start()
+
+            @pl.when(on(lax.rem(z + zs - step, zs)))
+            def _():
+                right_copy(step).start()
+
         if step < left_steps:
-            left_copy(step).start()
+
+            @pl.when(on(lax.rem(z + step, zs)))
+            def _():
+                left_copy(step).start()
 
     ring(0)
     h_pair[:, my_rows, :] = h_own[pl.ds(core, 1)].reshape(chips, CH, rows)
     h_copy.wait_recv()
     h_send[...] = h_pair[...].astype(BF16)
-    send_all(chips, me, h_send, h_recv, far_send.at[0], far_recv.at[0])
+    send_all(z, xh, h_send, h_recv, far_send.at[0], far_recv.at[0])
 
     x_load.wait()
     small[0].wait()
@@ -265,17 +310,17 @@
     halo_copy(0).wait_recv()
     features = []
     for s in range(3):
-        x = x_all[s].astype(F32)
-        first = jnp.where(me == 0, 0.0, x[:halo])
-        x = jnp.concatenate([first, x[halo:]], axis=0)
-        total = taps[s, 0:1, mine] * x[halo:]
+        raw = x_all[s].astype(F32)
+        first = jnp.where(me == 0, 0.0, raw[:halo])
+        raw = jnp.concatenate([first, raw[halo:]], axis=0)
+        total = taps[s, 0:1, mine] * raw[halo:]
         for back in range(1, taps.shape[1]):
-            total = total + taps[s, back : back + 1, mine] * x[halo - back : halo - back + 2 * rows]
+            total = total + taps[s, back : back + 1, mine] * raw[halo - back : halo - back + 2 * rows]
         features.append(total)
     query, mixed_in = features[0], features[1] * features[2]
     flipped = mixed_in.T.reshape(chips, CH, 2 * rows)
     u_send[...] = jnp.concatenate([flipped[:, :, :rows], flipped[:, :, rows:]], axis=1).astype(BF16)
-    send_all(chips, me, u_send, u_recv, far_send.at[1], far_recv.at[1])
+    send_all(z, xh, u_send, u_recv, far_send.at[1], far_recv.at[1])
     ring(1)
 
     for load in small[1:]:
@@ -300,91 +345,116 @@
     product = jnp.concatenate([h_re * u_im + h_im * u_re, h_re * u_re - h_im * u_im], axis=1)
     inverse(product, scratch, t_re, t_im, b_dft, a_inv)
     y_send[...] = scratch[...].reshape(y_send.shape).astype(BF16)
-    send_all(chips, me, y_send, y_recv, far_send.at[2], far_recv.at[2])
-    ring(6)
-    ring(7)
+    send_all(z, xh, y_send, y_recv, far_send.at[2], far_recv.at[2])
     wait_all(chips, y_recv, far_recv.at[2])
-    for step in range(8, right_steps + 1):
-        ring(step)
     back = y_recv[...].astype(F32)
     convolved = jnp.concatenate(
         [back[:, CH * b : CH * (b + 1), :].reshape(half, rows).T for b in range(2)], axis=0
     )
     gated[...] = (query * (convolved + skip[:, mine] * mixed_in)).astype(BF16)
 
-    copies = []
-    for far in range(2):
-        for cross in range(2):
-            if far == 0 and cross == 0:
-                continue
-            index = far * 2 + cross - 1
-            copies.append(
-                pltpu.make_async_remote_copy(
-                    src_ref=gated,
-                    dst_ref=g_all.at[xh, :, mine],
-                    send_sem=g_send.at[index],
-                    recv_sem=g_recv.at[index],
-                    device_id={"xh": 1 - xh if far else xh, "core": other if cross else core},
-                )
-            )
-    for copy in copies:
-        copy.start()
     tokens = 2 * rows
-    g_all[pl.ds(xh, 1), :, mine] = gated[...].reshape(1, tokens, half)
-    per_owner = zs // groups
-    columns = weight.shape[1]
+
+    def g_at(ref, which):
+        return ref.at[which // 2, lax.rem(which, 2), :, mine]
+
+    def g_copy(index, source, which, device_id):
+        return pltpu.make_async_remote_copy(
+            src_ref=source,
+            dst_ref=g_at(g_all, which),
+            send_sem=g_send.at[index],
+            recv_sem=g_recv.at[index],
+            device_id=device_id,
+        )
+
+    across = lax.rem(x + 2, 4)
+    to_up = g_copy(0, gated, x, up_x)
+    to_down = g_copy(1, gated, x, down_x)
+    to_other = [
+        g_copy(3, gated, x, {"core": other}),
+        g_copy(4, g_at(g_all, down), down, {"core": other}),
+        g_copy(5, g_at(g_all, up), up, {"core": other}),
+        g_copy(6, g_at(g_all, across), across, {"core": other}),
+    ]
+    pass_up = g_copy(2, g_at(g_all, down), down, up_x)
+    pass_down = g_copy(2, g_at(g_all, up), up, down_x)
+    to_up.start()
+    to_down.start()
+    to_other[0].start()
+    g_all[pl.ds(xh, 1), pl.ds(xl, 1), :, mine] = gated[...].reshape(1, 1, tokens, half)
+    for step in range(6, right_steps + 1):
+        ring(step)
+    to_up.wait_recv()
+    to_other[1].start()
+
+    @pl.when(core == 0)
+    def _():
+        pass_up.start()
+
+    to_down.wait_recv()
+    to_other[2].start()
+
+    @pl.when(core == 1)
+    def _():
+        pass_down.start()
+
+    columns = weight.shape[2]
     wide = per_owner * columns
 
     def send(which_x, b, owner):
         pltpu.make_async_remote_copy(
             src_ref=parts.at[which_x, b, owner],
-            dst_ref=landed.at[slot, owner_me],
+            dst_ref=landed.at[slot, y],
             send_sem=part_send,
-            recv_sem=part_recv.at[slot, owner_me],
-            device_id={"xh": which_x, "core": b, "y": owner // xls, "xl": lax.rem(owner, xls)},
+            recv_sem=part_recv.at[slot, y],
+            device_id={"xh": which_x, "core": b, "y": owner},
         ).start()
 
     def compute(which_x, owner):
-        block = weight[pl.ds(owner * per_owner, per_owner)].reshape(wide, 2 * half)
-        left = g_all[pl.ds(which_x, 1)].reshape(tokens, 2 * half)
-        product = lax.dot_general(
-            left, block, (((1,), (1,)), ((), ())), preferred_element_type=F32
-        ).astype(BF16)
+        product = jnp.zeros((tokens, wide), F32)
+        for part in range(2):
+            block = weight[pl.ds(owner * per_owner, per_owner), part].reshape(wide, 2 * half)
+            left = g_all[pl.ds(which_x, 1), part].reshape(tokens, 2 * half)
+            product = product + lax.dot_general(
+                left, block, (((1,), (1,)), ((), ())), preferred_element_type=F32
+            )
         for b in range(2):
-            parts[pl.ds(which_x, 1), b, pl.ds(owner, 1)] = product[
-                b * rows : (b + 1) * rows
-            ].reshape(1, 1, rows, wide)
-
-    copies[0].wait_recv()
+            parts[pl.ds(which_x, 1), b, pl.ds(owner, 1)] = (
+                product[b * rows : (b + 1) * rows].astype(BF16).reshape(1, 1, rows, wide)
+            )
+
+    for copy in to_other[:3]:
+        copy.wait_recv()
 
     def own_step(k, carry):
-        owner = lax.rem(owner_me + k, groups)
+        owner = lax.rem(y + k, ys)
         compute(xh, owner)
         for b in range(2):
             send(xh, b, owner)
         return carry
 
-    lax.fori_loop(1, groups, own_step, 0)
-    compute(xh, owner_me)
-    send(xh, other, owner_me)
-    landed[pl.ds(slot, 1), pl.ds(owner_me, 1)] = parts[
-        pl.ds(xh, 1), pl.ds(core, 1), pl.ds(owner_me, 1)
+    lax.fori_loop(1, ys, own_step, 0)
+    compute(xh, y)
+    send(xh, other, y)
+    landed[pl.ds(slot, 1), pl.ds(y, 1)] = parts[
+        pl.ds(xh, 1), pl.ds(core, 1), pl.ds(y, 1)
     ].reshape(1, 1, rows, wide)
-    copies[1].wait_recv()
-    copies[2].wait_recv()
+    pass_up.wait_recv()
+    to_other[3].start()
+    to_other[3].wait_recv()
 
     def far_step(k, carry):
-        owner = lax.rem(owner_me + k, groups)
+        owner = lax.rem(y + k, ys)
         compute(1 - xh, owner)
         for b in range(2):
             send(1 - xh, b, owner)
         return carry
 
-    lax.fori_loop(0, groups, far_step, 0)
+    lax.fori_loop(0, ys, far_step, 0)
 
     def arrived(k, carry):
         index = lax.rem(my_index + k, everyone)
-        which, owner = index // groups, lax.rem(index, groups)
+        which, owner = index // ys, lax.rem(index, ys)
         block = landed.at[which, owner]
         pltpu.make_async_copy(block, block, part_recv.at[which, owner]).wait()
         return carry
@@ -393,7 +463,7 @@
     sums = []
     for s in range(4):
         total = landed[s, 0].astype(F32)
-        for owner in range(1, groups):
+        for owner in range(1, ys):
             total = total + landed[s, owner].astype(F32)
         sums.append(total)
     for part in range(per_owner):
@@ -410,16 +480,28 @@
         halo_copy(0).wait_send()
         halo_copy(1).wait_send()
 
+    @pl.when(jnp.logical_not(on(z)))
+    def _():
+        swap.wait_send()
+
     for step in range(right_steps):
-        right_copy(step).wait_send()
+
+        @pl.when(on(lax.rem(z + zs - step, zs)))
+        def _():
+            right_copy(step).wait_send()
+
     for step in range(left_steps):
-        left_copy(step).wait_send()
+
+        @pl.when(on(lax.rem(z + step, zs)))
+        def _():
+            left_copy(step).wait_send()
+
     wait_all(chips, h_send, far_send.at[0])
     wait_all(chips, u_send, far_send.at[1])
     wait_all(chips, y_send, far_send.at[2])
-    for copy in copies:
+    for copy in (to_up, to_down, pass_up, *to_other):
         copy.wait_send()
-    for sent in (parts.at[0, 0, pl.ds(0, groups - 1)], parts.at[0, 1], parts.at[1]):
+    for sent in (parts.at[0, 0, pl.ds(0, ys - 1)], parts.at[0, 1], parts.at[1]):
         pltpu.make_async_copy(sent, sent, part_send).wait()
 
 
@@ -428,10 +510,10 @@
     half = channels // 2
     zs = lax.axis_size("z")
     chips = zs * 2
-    groups = lax.axis_size("y") * lax.axis_size("xl")
+    ys = lax.axis_size("y")
     blocks = 2 * chips
     columns = out_weight.shape[1]
-    wide = zs // groups * columns
+    wide = zs // (2 * ys) * columns
     lookup = tables(blocks, rows)
     exchange = (chips, 2 * CH, rows)
     dma = pltpu.SemaphoreType.DMA
@@ -458,24 +540,24 @@
             pltpu.VMEM(exchange, BF16),
             pltpu.VMEM(exchange, BF16),
             pltpu.VMEM((blocks * CH, rows), F32),
-            pltpu.VMEM((zs, columns, channels), BF16),
+            pltpu.VMEM((zs // 2, 2, columns, channels), BF16),
             pltpu.VMEM((2 * rows, half), BF16),
-            pltpu.VMEM((2, 2 * rows, channels), BF16),
-            pltpu.VMEM((2, 2, groups, rows, wide), BF16),
-            pltpu.VMEM((4, groups, rows, wide), BF16),
+            pltpu.VMEM((2, 2, 2 * rows, channels), BF16),
+            pltpu.VMEM((2, 2, ys, rows, wide), BF16),
+            pltpu.VMEM((4, ys, rows, wide), BF16),
             dma((9,)),
+            dma((5,)),
             dma((4,)),
-            dma((3,)),
             dma((3,)),
             dma((3,)),
             dma((zs,)),
             dma((zs,)),
             dma((zs,)),
             dma((zs,)),
-            dma((3,)),
-            dma((3,)),
+            dma((7,)),
+            dma((7,)),
             dma,
-            dma((4, groups)),
+            dma((4, ys)),
         ],
         compiler_params=pltpu.CompilerParams(
             collective_id=0, has_side_effects=True, vmem_limit_bytes=60 * 2**20

time: 85 us -> 92.6 us (1.089)
  Pallas kernels: 83.3 us -> 90.9 us
    pallas_call x1, Pallas kernels: 83.3 us -> 90.9 us  [body(): pl.pallas_call(mixer_kernel, out_shape=jax.ShapeDtypeStruct((rows, channe...]
where the time goes in v4:
time: 92.6 us; the launch traced here: 92.4 us
  Pallas kernels  90.9 us (98%)
  local copies, waits for them, and re-layouts  1.57 us (2%)
    pallas_call x1, Pallas kernels, body(): pl.pallas_call(mixer_kernel, out_shape=jax.ShapeDtypeStruct((rows, channe...  90.9 us

profile of v4, /device:TPU:1, one launch (start us, length us, event | category | flops | bytes accessed | tf_op | source)
XLA Modules:
  0.0 92.4 jit_solution(2741377013234575186)
XLA Ops:
  0.0 90.9 %mixer.1 = bf16[128,512]{1,0:T(8,128)(2,1)} custom-call(bf16[3,128,512]{2,1,0:T(8,128)(2,1)} %bitcast.3, f32[3,3,512]{2,1,0:T(4,128)} %taps_hbm.1, f32[128,512]{1,0:T(8,128)} %filt_hbm.1, f32[1,512]{1,0:T(1,128)} %bitcast.5, bf16[64,512]{1,0:T(8,128)(2,1)} %bitcast.4, f32[128,64]{1,0:T(8,128)} %constant.8.clone.a_fwd_hbm, ...), custom_call_target="tpu_custom_call" | custom-call | tf_op jit(solution)/shard_map/mixer/pallas_call | solution.py:520
  90.9 1.6 %copy.11 = bf16[128,512]{1,0:T(8,128)(2,1)} copy(bf16[128,512]{1,0:T(8,128)(2,1)} %mixer.1) | data formatting | bytes 262144

commit v5 on v4

--- a/solution.py
+++ b/solution.py
@@ -37,9 +37,10 @@
     return high, (value - high.astype(F32)).astype(BF16)
 
 
-def send_all(z, xh, source, target, send_sem, recv_sem):
+def send_all(z, xh, source, target, send_sem, recv_sems):
     zs = lax.axis_size("z")
     me = z * 2 + xh
+    size = 2 * zs // recv_sems.shape[0]
 
     def step(k, carry):
         turn = k // 2
@@ -50,7 +51,7 @@
             src_ref=source.at[to_z * 2 + to_x],
             dst_ref=target.at[me],
             send_sem=send_sem,
-            recv_sem=recv_sem,
+            recv_sem=recv_sems.at[k // size],
             device_id={"z": to_z, "xh": to_x},
         ).start()
         return carry
@@ -59,9 +60,14 @@
     target[pl.ds(me, 1)] = source[pl.ds(me, 1)]
 
 
-def wait_all(chips, ref, sem):
-    part = ref.at[pl.ds(0, chips - 1)]
+def wait_blocks(count, ref, sem):
+    part = ref.at[pl.ds(0, count)]
     pltpu.make_async_copy(part, part, sem).wait()
+
+
+def wait_group(ref, sems, group):
+    size = ref.shape[0] // sems.shape[0]
+    wait_blocks(size - (group == sems.shape[0] - 1), ref, sems.at[group])
 
 
 def spectrum(received, scratch, a_fwd, t_re, t_im, b_dft):
@@ -126,7 +132,6 @@
     chips = zs * 2
     per_owner = zs // (2 * ys)
     me = z * 2 + xh
-    slot = xh * 2 + core
     other = 1 - core
     rows = qkv_hbm.shape[1]
     half = chips * CH
@@ -134,27 +139,21 @@
     mine = pl.ds(pl.multiple_of(core * half, half), half)
     theirs = pl.ds(pl.multiple_of(other * half, half), half)
     place = pl.ds(pl.multiple_of(halo + core * rows, 16), rows)
-    everyone = 4 * ys
-    my_index = slot * ys + y
     x = xh * 2 + xl
+    everyone = 8 * ys
+    my_index = (x * 2 + core) * ys + y
     up, down = lax.rem(x + 1, 4), lax.rem(x + 3, 4)
     up_x = {"xh": up // 2, "xl": lax.rem(up, 2)}
     down_x = {"xh": down // 2, "xl": lax.rem(down, 2)}
-
-    def on(block):
-        return lax.rem(block // per_owner, 2) == xl
-
-    def spot(block):
-        return block // (2 * per_owner) * per_owner + lax.rem(block, per_owner)
+    columns = weight.shape[2]
 
     filt_load = local_copy(filt_hbm, filt, load_sem.at[0])
     x_load = local_copy(qkv_hbm.at[:, :, mine], x_all.at[:, place, :], load_sem.at[1])
-    weight_load = pltpu.make_async_copy(weight_hbm, weight.at[spot(z), xl], load_sem.at[2])
-
-    @pl.when(on(z))
-    def _():
-        weight_load.start()
-
+    weight_load = local_copy(
+        weight_hbm.at[pl.ds(pl.multiple_of(xl * columns, columns), columns), :],
+        weight.at[z, xl],
+        load_sem.at[2],
+    )
     small = [
         local_copy(source, target, load_sem.at[3 + k])
         for k, (source, target) in enumerate(
@@ -175,12 +174,15 @@
         barrier, inc=1, device_id={"z": step_to // 2, "xh": lax.rem(step_to, 2), "core": other}
     )
 
-    pl.semaphore_signal(barrier, inc=1, device_id=up_x)
-    pl.semaphore_signal(barrier, inc=1, device_id=down_x)
 
     def place_of(index):
         which = index // ys
-        return {"xh": which // 2, "core": lax.rem(which, 2), "y": lax.rem(index, ys)}
+        return {
+            "xh": which // 4,
+            "xl": lax.rem(which // 2, 2),
+            "core": lax.rem(which, 2),
+            "y": lax.rem(index, ys),
+        }
 
     def greet_ctx(k, carry):
         peer = lax.rem(me + k, chips)
@@ -198,7 +200,7 @@
 
     filt_load.wait()
     h_own[...] = filt[...].T.reshape(2, chips, CH, rows)
-    pl.semaphore_wait(barrier, 3 + chips - 1 + everyone - 1)
+    pl.semaphore_wait(barrier, 1 + chips - 1 + everyone - 1)
 
     my_rows = pl.ds(pl.multiple_of(core * CH, CH), CH)
     h_copy = pltpu.make_async_remote_copy(
@@ -235,24 +237,20 @@
         halo_copy(1).start()
 
     swap = pltpu.make_async_remote_copy(
-        src_ref=weight_hbm,
-        dst_ref=weight.at[spot(z), xl],
+        src_ref=weight_hbm.at[pl.ds(pl.multiple_of((1 - xl) * columns, columns), columns), :],
+        dst_ref=weight.at[z, xl],
         send_sem=near_send.at[4],
         recv_sem=near_recv.at[3],
         device_id={"xl": 1 - xl},
     )
-
-    @pl.when(jnp.logical_not(on(z)))
-    def _():
-        swap.start()
-
+    swap.start()
     right_steps = zs // 2
     left_steps = zs - 1 - right_steps
 
     def pass_on(block, step, send_sem, recv_sem, ahead):
         return pltpu.make_async_remote_copy(
-            src_ref=weight.at[spot(block)],
-            dst_ref=weight.at[spot(block)],
+            src_ref=weight.at[block],
+            dst_ref=weight.at[block],
             send_sem=send_sem.at[step],
             recv_sem=recv_sem.at[step],
             device_id={"z": lax.rem(z + ahead, zs)},
@@ -265,44 +263,29 @@
         return pass_on(lax.rem(z + step, zs), step, left_send, left_recv, zs - 1)
 
     def landing(step, shift, sem):
-        block = lax.rem(z + shift, zs)
-
-        @pl.when(on(block))
-        def _():
-            landed_at = weight.at[spot(block)]
-            pltpu.make_async_copy(landed_at, landed_at, sem.at[step]).wait()
+        landed_at = weight.at[lax.rem(z + shift, zs)]
+        pltpu.make_async_copy(landed_at, landed_at, sem.at[step]).wait()
 
     def ring(step):
         if step > right_steps:
             return
         if step == 0:
-
-            @pl.when(on(z))
-            def _():
-                weight_load.wait()
-                swap.wait_recv()
-
+            weight_load.wait()
+            swap.wait_recv()
         if 0 < step <= right_steps:
             landing(step - 1, zs - step, right_recv)
         if 0 < step <= left_steps:
             landing(step - 1, step, left_recv)
         if step < right_steps:
-
-            @pl.when(on(lax.rem(z + zs - step, zs)))
-            def _():
-                right_copy(step).start()
-
+            right_copy(step).start()
         if step < left_steps:
-
-            @pl.when(on(lax.rem(z + step, zs)))
-            def _():
-                left_copy(step).start()
-
-    ring(0)
+            left_copy(step).start()
+
     h_pair[:, my_rows, :] = h_own[pl.ds(core, 1)].reshape(chips, CH, rows)
     h_copy.wait_recv()
     h_send[...] = h_pair[...].astype(BF16)
     send_all(z, xh, h_send, h_recv, far_send.at[0], far_recv.at[0])
+    ring(0)
 
     x_load.wait()
     small[0].wait()
@@ -330,15 +313,16 @@
     b_dft[...] = jnp.concatenate([high, high, low], axis=0)
     high, low = high_low(a_back[...])
     a_inv[...] = jnp.concatenate([high, high, low], axis=1)
-    wait_all(chips, h_recv, far_recv.at[0])
+    for group in range(4):
+        wait_group(h_recv, far_recv.at[0], group)
     ring(2)
     t_re, t_im = t_both[0], t_both[1]
     h_freq = spectrum(h_recv, scratch, a_fwd, t_re, t_im, b_dft)
-    ring(3)
-    wait_all(chips, u_recv, far_recv.at[1])
-    ring(4)
+    for group in range(4):
+        wait_group(u_recv, far_recv.at[1], group)
+        if group == 1:
+            ring(3)
     u_freq = spectrum(u_recv, scratch, a_fwd, t_re, t_im, b_dft)
-    ring(5)
     width = t_re.shape[1]
     h_re, h_im = h_freq[:, :width], h_freq[:, width:]
     u_re, u_im = u_freq[:, :width], u_freq[:, width:]
@@ -346,108 +330,130 @@
     inverse(product, scratch, t_re, t_im, b_dft, a_inv)
     y_send[...] = scratch[...].reshape(y_send.shape).astype(BF16)
     send_all(z, xh, y_send, y_recv, far_send.at[2], far_recv.at[2])
-    wait_all(chips, y_recv, far_recv.at[2])
+    ring(4)
+    for group in range(4):
+        wait_group(y_recv, far_recv.at[2], group)
+        if group == 1:
+            ring(5)
     back = y_recv[...].astype(F32)
     convolved = jnp.concatenate(
         [back[:, CH * b : CH * (b + 1), :].reshape(half, rows).T for b in range(2)], axis=0
     )
-    gated[...] = (query * (convolved + skip[:, mine] * mixed_in)).astype(BF16)
-
+    across = lax.rem(x + 2, 4)
+
+    def g_copy(kind, b, source, which, device_id):
+        def at(ref):
+            return ref.at[which // 2, lax.rem(which, 2), pl.ds(b * rows, rows), mine]
+
+        return pltpu.make_async_remote_copy(
+            src_ref=gated.at[pl.ds(b * rows, rows), :] if source is gated else at(source),
+            dst_ref=at(g_all),
+            send_sem=g_send.at[kind, b],
+            recv_sem=g_recv.at[kind, b],
+            device_id=device_id,
+        )
+
+    to_up = [g_copy(0, b, gated, x, up_x) for b in range(2)]
+    to_down = [g_copy(1, b, gated, x, down_x) for b in range(2)]
+    pass_up = [g_copy(2, b, g_all, down, up_x) for b in range(2)]
+    pass_down = [g_copy(2, b, g_all, up, down_x) for b in range(2)]
+    share = [g_copy(3, b, gated, x, {"core": other}) for b in range(2)]
+    share_down = [g_copy(4, b, g_all, down, {"core": other}) for b in range(2)]
+    share_up = [g_copy(5, b, g_all, up, {"core": other}) for b in range(2)]
+    share_across = [g_copy(6, b, g_all, across, {"core": other}) for b in range(2)]
+    for b in range(2):
+        part = slice(b * rows, (b + 1) * rows)
+        value = (query[part] * (convolved[part] + skip[:, mine] * mixed_in[part])).astype(BF16)
+        gated[part, :] = value
+        g_all[pl.ds(xh, 1), pl.ds(xl, 1), part, mine] = value.reshape(1, 1, rows, half)
+        to_up[b].start()
+        to_down[b].start()
+        share[b].start()
+    ring(6)
+    for b in range(2):
+        to_up[b].wait_recv()
+        share_down[b].start()
+
+        @pl.when(core == 0)
+        def _():
+            pass_up[b].start()
+
+        to_down[b].wait_recv()
+        share_up[b].start()
+
+        @pl.when(core == 1)
+        def _():
+            pass_down[b].start()
+
+    ring(7)
+    for b in range(2):
+        pass_up[b].wait_recv()
+        share_across[b].start()
+    for step in range(8, right_steps + 1):
+        ring(step)
     tokens = 2 * rows
-
-    def g_at(ref, which):
-        return ref.at[which // 2, lax.rem(which, 2), :, mine]
-
-    def g_copy(index, source, which, device_id):
-        return pltpu.make_async_remote_copy(
-            src_ref=source,
-            dst_ref=g_at(g_all, which),
-            send_sem=g_send.at[index],
-            recv_sem=g_recv.at[index],
-            device_id=device_id,
-        )
-
-    across = lax.rem(x + 2, 4)
-    to_up = g_copy(0, gated, x, up_x)
-    to_down = g_copy(1, gated, x, down_x)
-    to_other = [
-        g_copy(3, gated, x, {"core": other}),
-        g_copy(4, g_at(g_all, down), down, {"core": other}),
-        g_copy(5, g_at(g_all, up), up, {"core": other}),
-        g_copy(6, g_at(g_all, across), across, {"core": other}),
-    ]
-    pass_up = g_copy(2, g_at(g_all, down), down, up_x)
-    pass_down = g_copy(2, g_at(g_all, up), up, down_x)
-    to_up.start()
-    to_down.start()
-    to_other[0].start()
-    g_all[pl.ds(xh, 1), pl.ds(xl, 1), :, mine] = gated[...].reshape(1, 1, tokens, half)
-    for step in range(6, right_steps + 1):
-        ring(step)
-    to_up.wait_recv()
-    to_other[1].start()
-
-    @pl.when(core == 0)
-    def _():
-        pass_up.start()
-
-    to_down.wait_recv()
-    to_other[2].start()
-
-    @pl.when(core == 1)
-    def _():
-        pass_down.start()
-
-    columns = weight.shape[2]
     wide = per_owner * columns
 
-    def send(which_x, b, owner):
+    def send(which_x, b, to_y, to_x):
         pltpu.make_async_remote_copy(
-            src_ref=parts.at[which_x, b, owner],
-            dst_ref=landed.at[slot, y],
+            src_ref=parts.at[which_x, b, to_y, to_x],
+            dst_ref=landed.at[x * 2 + core, y],
             send_sem=part_send,
-            recv_sem=part_recv.at[slot, y],
-            device_id={"xh": which_x, "core": b, "y": owner},
+            recv_sem=part_recv.at[x * 2 + core, y],
+            device_id={"xh": which_x, "xl": to_x, "core": b, "y": to_y},
         ).start()
 
-    def compute(which_x, owner):
-        product = jnp.zeros((tokens, wide), F32)
+    def compute(which_x, to_y):
+        product = jnp.zeros((2 * wide, tokens), F32)
         for part in range(2):
-            block = weight[pl.ds(owner * per_owner, per_owner), part].reshape(wide, 2 * half)
-            left = g_all[pl.ds(which_x, 1), part].reshape(tokens, 2 * half)
+            block = weight[pl.ds(to_y * 2 * per_owner, 2 * per_owner), part]
+            right = g_all[pl.ds(which_x, 1), part].reshape(tokens, 2 * half)
             product = product + lax.dot_general(
-                left, block, (((1,), (1,)), ((), ())), preferred_element_type=F32
+                block.reshape(2 * wide, 2 * half),
+                right,
+                (((1,), (1,)), ((), ())),
+                preferred_element_type=F32,
             )
         for b in range(2):
-            parts[pl.ds(which_x, 1), b, pl.ds(owner, 1)] = (
-                product[b * rows : (b + 1) * rows].astype(BF16).reshape(1, 1, rows, wide)
+            parts[pl.ds(which_x, 1), b, pl.ds(to_y, 1)] = (
+                product[:, b * rows : (b + 1) * rows]
+                .astype(BF16)
+                .reshape(1, 1, 2, wide, rows)
             )
 
-    for copy in to_other[:3]:
-        copy.wait_recv()
+    for b in range(2):
+        share[b].wait_recv()
+        share_down[b].wait_recv()
+        share_up[b].wait_recv()
+
+    def own_last():
+        compute(xh, y)
+        send(xh, core, y, 1 - xl)
+        send(xh, other, y, xl)
+        send(xh, other, y, 1 - xl)
+        landed[pl.ds(x * 2 + core, 1), pl.ds(y, 1)] = parts[
+            pl.ds(xh, 1), pl.ds(core, 1), pl.ds(y, 1), pl.ds(xl, 1)
+        ].reshape(1, 1, wide, rows)
 
     def own_step(k, carry):
-        owner = lax.rem(y + k, ys)
-        compute(xh, owner)
+        to_y = lax.rem(y + k, ys)
+        compute(xh, to_y)
         for b in range(2):
-            send(xh, b, owner)
+            for to_x in range(2):
+                send(xh, b, to_y, to_x)
         return carry
 
     lax.fori_loop(1, ys, own_step, 0)
-    compute(xh, y)
-    send(xh, other, y)
-    landed[pl.ds(slot, 1), pl.ds(y, 1)] = parts[
-        pl.ds(xh, 1), pl.ds(core, 1), pl.ds(y, 1)
-    ].reshape(1, 1, rows, wide)
-    pass_up.wait_recv()
-    to_other[3].start()
-    to_other[3].wait_recv()
+    own_last()
+    for b in range(2):
+        share_across[b].wait_recv()
 
     def far_step(k, carry):
-        owner = lax.rem(y + k, ys)
-        compute(1 - xh, owner)
+        to_y = lax.rem(y + k, ys)
+        compute(1 - xh, to_y)
         for b in range(2):
-            send(1 - xh, b, owner)
+            for to_x in range(2):
+                send(1 - xh, b, to_y, to_x)
         return carry
 
     lax.fori_loop(0, ys, far_step, 0)
@@ -461,16 +467,18 @@
 
     lax.fori_loop(1, everyone, arrived, 0)
     sums = []
-    for s in range(4):
-        total = landed[s, 0].astype(F32)
-        for owner in range(1, ys):
-            total = total + landed[s, owner].astype(F32)
+    for which in range(8):
+        total = landed[which, 0].astype(F32)
+        for source in range(1, ys):
+            total = total + landed[which, source].astype(F32)
         sums.append(total)
-    for part in range(per_owner):
-        pieces = [total[:, part * columns : (part + 1) * columns] for total in sums]
-        out[:, part * 4 * columns : (part + 1) * 4 * columns] = jnp.concatenate(
-            pieces, axis=1
-        ).astype(out.dtype)
+    order = [a * 4 + c * 2 + b for a in range(2) for b in range(2) for c in range(2)]
+    pieces = [
+        sums[which][part * columns : (part + 1) * columns]
+        for part in range(per_owner)
+        for which in order
+    ]
+    out[...] = jnp.concatenate(pieces, axis=0).T.astype(out.dtype)
 
     h_copy.wait_send()
     x_copy.wait_send()
@@ -480,28 +488,22 @@
         halo_copy(0).wait_send()
         halo_copy(1).wait_send()
 
-    @pl.when(jnp.logical_not(on(z)))
-    def _():
-        swap.wait_send()
-
+    swap.wait_send()
     for step in range(right_steps):
-
-        @pl.when(on(lax.rem(z + zs - step, zs)))
-        def _():
-            right_copy(step).wait_send()
-
+        right_copy(step).wait_send()
     for step in range(left_steps):
-
-        @pl.when(on(lax.rem(z + step, zs)))
-        def _():
-            left_copy(step).wait_send()
-
-    wait_all(chips, h_send, far_send.at[0])
-    wait_all(chips, u_send, far_send.at[1])
-    wait_all(chips, y_send, far_send.at[2])
-    for copy in (to_up, to_down, pass_up, *to_other):
-        copy.wait_send()
-    for sent in (parts.at[0, 0, pl.ds(0, ys - 1)], parts.at[0, 1], parts.at[1]):
+        left_copy(step).wait_send()
+    wait_blocks(chips - 1, h_send, far_send.at[0])
+    wait_blocks(chips - 1, u_send, far_send.at[1])
+    wait_blocks(chips - 1, y_send, far_send.at[2])
+    for group in (to_up, to_down, pass_up, share, share_down, share_up, share_across):
+        for copy in group:
+            copy.wait_send()
+    pltpu.make_async_copy(parts.at[1], parts.at[1], part_send).wait()
+    pltpu.make_async_copy(parts.at[0, 1], parts.at[0, 1], part_send).wait()
+    pltpu.make_async_copy(parts.at[0, 0, 0, 0], parts.at[0, 0, 0, 0], part_send).wait()
+    if ys > 1:
+        sent = parts.at[0, 0, pl.ds(1, ys - 1)]
         pltpu.make_async_copy(sent, sent, part_send).wait()
 
 
@@ -512,7 +514,7 @@
     chips = zs * 2
     ys = lax.axis_size("y")
     blocks = 2 * chips
-    columns = out_weight.shape[1]
+    columns = out_weight.shape[1] // 2
     wide = zs // (2 * ys) * columns
     lookup = tables(blocks, rows)
     exchange = (chips, 2 * CH, rows)
@@ -540,24 +542,24 @@
             pltpu.VMEM(exchange, BF16),
             pltpu.VMEM(exchange, BF16),
             pltpu.VMEM((blocks * CH, rows), F32),
-            pltpu.VMEM((zs // 2, 2, columns, channels), BF16),
+            pltpu.VMEM((zs, 2, columns, channels), BF16),
             pltpu.VMEM((2 * rows, half), BF16),
             pltpu.VMEM((2, 2, 2 * rows, channels), BF16),
-            pltpu.VMEM((2, 2, ys, rows, wide), BF16),
-            pltpu.VMEM((4, ys, rows, wide), BF16),
+            pltpu.VMEM((2, 2, ys, 2, wide, rows), BF16),
+            pltpu.VMEM((8, ys, wide, rows), BF16),
             dma((9,)),
             dma((5,)),
             dma((4,)),
             dma((3,)),
-            dma((3,)),
+            dma((3, 4)),
             dma((zs,)),
             dma((zs,)),
             dma((zs,)),
             dma((zs,)),
-            dma((7,)),
-            dma((7,)),
+            dma((7, 2)),
+            dma((7, 2)),
             dma,
-            dma((4, ys)),
+            dma((8, ys)),
         ],
         compiler_params=pltpu.CompilerParams(
             collective_id=0, has_side_effects=True, vmem_limit_bytes=60 * 2**20

time: 92.6 us -> 76.7 us (0.83)
  Pallas kernels: 90.9 us -> 75 us
    pallas_call x1, Pallas kernels: 90.9 us -> 75 us  [body(): pl.pallas_call(mixer_kernel, out_shape=jax.ShapeDtypeStruct((rows, channe...]
where the time goes in v5:
time: 76.7 us; the launch traced here: 76.6 us
  Pallas kernels  75 us (98%)
  local copies, waits for them, and re-layouts  1.57 us (2%)
    pallas_call x1, Pallas kernels, body(): pl.pallas_call(mixer_kernel, out_shape=jax.ShapeDtypeStruct((rows, channe...  75 us
    unnamed x1, local copies, waits for them, and re-layouts  1.57 us

profile of v5, /device:TPU:1, one launch (start us, length us, event | category | flops | bytes accessed | tf_op | source)
XLA Modules:
  0.0 76.6 jit_solution(15630506190152479757)
XLA Ops:
  0.0 75.0 %mixer.1 = bf16[128,512]{1,0:T(8,128)(2,1)} custom-call(bf16[3,128,512]{2,1,0:T(8,128)(2,1)} %bitcast.3, f32[3,3,512]{2,1,0:T(4,128)} %taps_hbm.1, f32[128,512]{1,0:T(8,128)} %filt_hbm.1, f32[1,512]{1,0:T(1,128)} %bitcast.5, bf16[64,512]{1,0:T(8,128)(2,1)} %bitcast.4, f32[128,64]{1,0:T(8,128)} %constant.8.clone.a_fwd_hbm, ...), custom_call_target="tpu_custom_call" | custom-call | tf_op jit(solution)/shard_map/mixer/pallas_call | solution.py:522
  75.0 1.6 %copy.11 = bf16[128,512]{1,0:T(8,128)(2,1)} copy(bf16[128,512]{1,0:T(8,128)(2,1)} %mixer.1) | data formatting | bytes 262144

commit v6 on v5

--- a/solution.py
+++ b/solution.py
@@ -37,7 +37,7 @@
     return high, (value - high.astype(F32)).astype(BF16)
 
 
-def send_all(z, xh, source, target, send_sem, recv_sems):
+def send_all(z, xh, source, target, send_sem, recv_sems, by_turn=False):
     zs = lax.axis_size("z")
     me = z * 2 + xh
     size = 2 * zs // recv_sems.shape[0]
@@ -49,7 +49,7 @@
         to_x = jnp.where(lax.rem(k, 2) == 0, 1 - xh, xh)
         pltpu.make_async_remote_copy(
             src_ref=source.at[to_z * 2 + to_x],
-            dst_ref=target.at[me],
+            dst_ref=target.at[turn * 2 + xh if by_turn else me],
             send_sem=send_sem,
             recv_sem=recv_sems.at[k // size],
             device_id={"z": to_z, "xh": to_x},
@@ -57,7 +57,8 @@
         return carry
 
     lax.fori_loop(0, 2 * zs - 1, step, 0)
-    target[pl.ds(me, 1)] = source[pl.ds(me, 1)]
+    slot = (zs - 1) * 2 + xh if by_turn else me
+    target[pl.ds(slot, 1)] = source[pl.ds(me, 1)]
 
 
 def wait_blocks(count, ref, sem):
@@ -122,7 +123,7 @@
     out,
     taps, filt, skip, a_table, t_both, b_table, a_back, a_fwd, b_dft, a_inv,
     h_own, h_pair, h_send, h_recv, x_all, u_send, u_recv, y_send, y_recv, scratch,
-    weight, gated, g_all, parts, landed,
+    weight, query_t, skip_t, g_all, g_ordered, parts, landed,
     load_sem, near_send, near_recv, far_send, far_recv,
     right_send, right_recv, left_send, left_recv, g_send, g_recv, part_send, part_recv,
 ):
@@ -289,6 +290,7 @@
 
     x_load.wait()
     small[0].wait()
+    small[1].wait()
     x_copy.wait_recv()
     halo_copy(0).wait_recv()
     features = []
@@ -305,8 +307,10 @@
     u_send[...] = jnp.concatenate([flipped[:, :, :rows], flipped[:, :, rows:]], axis=1).astype(BF16)
     send_all(z, xh, u_send, u_recv, far_send.at[1], far_recv.at[1])
     ring(1)
-
-    for load in small[1:]:
+    query_t[...] = query.T
+    skip_t[...] = (skip[:, mine] * mixed_in).T
+
+    for load in small[2:]:
         load.wait()
     a_fwd[...] = jnp.concatenate(high_low(a_table[...]), axis=1)
     high, low = high_low(b_table[...])
@@ -329,134 +333,132 @@
     product = jnp.concatenate([h_re * u_im + h_im * u_re, h_re * u_re - h_im * u_im], axis=1)
     inverse(product, scratch, t_re, t_im, b_dft, a_inv)
     y_send[...] = scratch[...].reshape(y_send.shape).astype(BF16)
-    send_all(z, xh, y_send, y_recv, far_send.at[2], far_recv.at[2])
+    send_all(z, xh, y_send, y_recv, far_send.at[2], far_recv.at[2], by_turn=True)
     ring(4)
+
+    tokens = 2 * rows
+    turns = zs // 4
+    pairs = 2 * CH
+    across = lax.rem(x + 2, 4)
+
+    def g_copy(kind, group, which, device_id):
+        part = g_all.at[which // 2, lax.rem(which, 2), core, pl.ds(group * turns, turns)]
+        return pltpu.make_async_remote_copy(
+            src_ref=part,
+            dst_ref=part,
+            send_sem=g_send.at[kind, group],
+            recv_sem=g_recv.at[kind, group],
+            device_id=device_id,
+        )
+
+    def g_copies(kind, which, device_id):
+        return [g_copy(kind, group, which, device_id) for group in range(4)]
+
+    to_across = g_copies(0, x, {"xh": 1 - xh})
+    to_up = g_copies(1, x, up_x)
+    to_down = g_copies(2, x, down_x)
+    share = g_copies(3, x, {"core": other})
+    share_across = g_copies(4, across, {"core": other})
+    share_down = g_copies(5, down, {"core": other})
+    share_up = g_copies(6, up, {"core": other})
     for group in range(4):
         wait_group(y_recv, far_recv.at[2], group)
+        for turn in range(group * turns, (group + 1) * turns):
+            ahead = zs // 2 + (-((turn + 1) // 2) if turn % 2 else turn // 2)
+            source = pl.ds(pl.multiple_of(lax.rem(z + zs - ahead, zs) * pairs, pairs), pairs)
+            back = y_recv[pl.ds(2 * turn, 2)].astype(F32)
+            convolved = jnp.concatenate(
+                [back[:, CH * b : CH * (b + 1), :].reshape(pairs, rows) for b in range(2)], axis=1
+            )
+            value = query_t[source, :] * (convolved + skip_t[source, :])
+            g_all[pl.ds(xh, 1), pl.ds(xl, 1), pl.ds(core, 1), turn] = value.astype(BF16).reshape(
+                1, 1, 1, pairs, tokens
+            )
+        to_across[group].start()
+        to_up[group].start()
+        to_down[group].start()
+        share[group].start()
         if group == 1:
             ring(5)
-    back = y_recv[...].astype(F32)
-    convolved = jnp.concatenate(
-        [back[:, CH * b : CH * (b + 1), :].reshape(half, rows).T for b in range(2)], axis=0
-    )
-    across = lax.rem(x + 2, 4)
-
-    def g_copy(kind, b, source, which, device_id):
-        def at(ref):
-            return ref.at[which // 2, lax.rem(which, 2), pl.ds(b * rows, rows), mine]
-
-        return pltpu.make_async_remote_copy(
-            src_ref=gated.at[pl.ds(b * rows, rows), :] if source is gated else at(source),
-            dst_ref=at(g_all),
-            send_sem=g_send.at[kind, b],
-            recv_sem=g_recv.at[kind, b],
-            device_id=device_id,
-        )
-
-    to_up = [g_copy(0, b, gated, x, up_x) for b in range(2)]
-    to_down = [g_copy(1, b, gated, x, down_x) for b in range(2)]
-    pass_up = [g_copy(2, b, g_all, down, up_x) for b in range(2)]
-    pass_down = [g_copy(2, b, g_all, up, down_x) for b in range(2)]
-    share = [g_copy(3, b, gated, x, {"core": other}) for b in range(2)]
-    share_down = [g_copy(4, b, g_all, down, {"core": other}) for b in range(2)]
-    share_up = [g_copy(5, b, g_all, up, {"core": other}) for b in range(2)]
-    share_across = [g_copy(6, b, g_all, across, {"core": other}) for b in range(2)]
-    for b in range(2):
-        part = slice(b * rows, (b + 1) * rows)
-        value = (query[part] * (convolved[part] + skip[:, mine] * mixed_in[part])).astype(BF16)
-        gated[part, :] = value
-        g_all[pl.ds(xh, 1), pl.ds(xl, 1), part, mine] = value.reshape(1, 1, rows, half)
-        to_up[b].start()
-        to_down[b].start()
-        share[b].start()
     ring(6)
-    for b in range(2):
-        to_up[b].wait_recv()
-        share_down[b].start()
-
-        @pl.when(core == 0)
-        def _():
-            pass_up[b].start()
-
-        to_down[b].wait_recv()
-        share_up[b].start()
-
-        @pl.when(core == 1)
-        def _():
-            pass_down[b].start()
-
-    ring(7)
-    for b in range(2):
-        pass_up[b].wait_recv()
-        share_across[b].start()
-    for step in range(8, right_steps + 1):
-        ring(step)
-    tokens = 2 * rows
+    for group in range(4):
+        to_up[group].wait_recv()
+        share_down[group].start()
+        to_down[group].wait_recv()
+        share_up[group].start()
+        to_across[group].wait_recv()
+        share_across[group].start()
+
+    owners = 2 * ys
+    owner_me = y * 2 + xl
     wide = per_owner * columns
 
-    def send(which_x, b, to_y, to_x):
+    def order(which_x):
+        for part in range(2):
+            for c in range(2):
+                for block in range(zs):
+                    shift = lax.rem(z + zs - block, zs) - zs // 2
+                    turn = jnp.where(shift < 0, -2 * shift - 1, 2 * shift)
+                    start = c * half + block * pairs
+                    g_ordered[which_x, part, start : start + pairs, :] = g_all[
+                        which_x, part, c, pl.ds(turn, 1)
+                    ].reshape(pairs, tokens)
+
+    def compute(which_x, to):
+        product = jnp.zeros((wide, tokens), F32)
+        for part in range(2):
+            block = weight[pl.ds(to * per_owner, per_owner), part].reshape(wide, 2 * half)
+            right = g_ordered[pl.ds(which_x, 1), part].reshape(2 * half, tokens)
+            product = product + dot(block, right)
+        for b in range(2):
+            parts[pl.ds(which_x, 1), b, pl.ds(to, 1)] = (
+                product[:, b * rows : (b + 1) * rows].astype(BF16).reshape(1, 1, wide, rows)
+            )
+
+    def send(which_x, b, to):
         pltpu.make_async_remote_copy(
-            src_ref=parts.at[which_x, b, to_y, to_x],
+            src_ref=parts.at[which_x, b, to],
             dst_ref=landed.at[x * 2 + core, y],
             send_sem=part_send,
             recv_sem=part_recv.at[x * 2 + core, y],
-            device_id={"xh": which_x, "xl": to_x, "core": b, "y": to_y},
+            device_id={"xh": which_x, "xl": lax.rem(to, 2), "core": b, "y": to // 2},
         ).start()
 
-    def compute(which_x, to_y):
-        product = jnp.zeros((2 * wide, tokens), F32)
-        for part in range(2):
-            block = weight[pl.ds(to_y * 2 * per_owner, 2 * per_owner), part]
-            right = g_all[pl.ds(which_x, 1), part].reshape(tokens, 2 * half)
-            product = product + lax.dot_general(
-                block.reshape(2 * wide, 2 * half),
-                right,
-                (((1,), (1,)), ((), ())),
-                preferred_element_type=F32,
-            )
-        for b in range(2):
-            parts[pl.ds(which_x, 1), b, pl.ds(to_y, 1)] = (
-                product[:, b * rows : (b + 1) * rows]
-                .astype(BF16)
-                .reshape(1, 1, 2, wide, rows)
-            )
-
-    for b in range(2):
-        share[b].wait_recv()
-        share_down[b].wait_recv()
-        share_up[b].wait_recv()
-
-    def own_last():
-        compute(xh, y)
-        send(xh, core, y, 1 - xl)
-        send(xh, other, y, xl)
-        send(xh, other, y, 1 - xl)
-        landed[pl.ds(x * 2 + core, 1), pl.ds(y, 1)] = parts[
-            pl.ds(xh, 1), pl.ds(core, 1), pl.ds(y, 1), pl.ds(xl, 1)
-        ].reshape(1, 1, wide, rows)
-
-    def own_step(k, carry):
-        to_y = lax.rem(y + k, ys)
-        compute(xh, to_y)
-        for b in range(2):
-            for to_x in range(2):
-                send(xh, b, to_y, to_x)
-        return carry
-
-    lax.fori_loop(1, ys, own_step, 0)
-    own_last()
-    for b in range(2):
-        share_across[b].wait_recv()
-
-    def far_step(k, carry):
-        to_y = lax.rem(y + k, ys)
-        compute(1 - xh, to_y)
-        for b in range(2):
-            for to_x in range(2):
-                send(1 - xh, b, to_y, to_x)
-        return carry
-
-    lax.fori_loop(0, ys, far_step, 0)
+    def project(which_x, first, count):
+        def step(k, carry):
+            to = lax.rem(z // per_owner + owners + first + lax.rem(k + y, count), owners)
+            compute(which_x, to)
+            for b in range(2):
+                stays = (which_x == xh) & (b == core) & (to == owner_me)
+
+                @pl.when(jnp.logical_not(stays))
+                def _():
+                    send(which_x, b, to)
+
+                @pl.when(stays)
+                def _():
+                    landed[pl.ds(x * 2 + core, 1), pl.ds(y, 1)] = parts[
+                        pl.ds(which_x, 1), b, pl.ds(to, 1)
+                    ].reshape(1, 1, wide, rows)
+
+            return carry
+
+        lax.fori_loop(0, count, step, 0)
+
+    near = min(5, owners)
+    for group in range(4):
+        for copy in (share, share_down, share_up, share_across):
+            copy[group].wait_recv()
+    order(0)
+    order(1)
+    project(1 - xh, -(near // 2), near)
+    project(xh, -(near // 2), near)
+    ring(7)
+    for step in range(8, right_steps + 1):
+        ring(step)
+    if near < owners:
+        project(1 - xh, near - near // 2, owners - near)
+        project(xh, near - near // 2, owners - near)
 
     def arrived(k, carry):
         index = lax.rem(my_index + k, everyone)
@@ -496,15 +498,13 @@
     wait_blocks(chips - 1, h_send, far_send.at[0])
     wait_blocks(chips - 1, u_send, far_send.at[1])
     wait_blocks(chips - 1, y_send, far_send.at[2])
-    for group in (to_up, to_down, pass_up, share, share_down, share_up, share_across):
+    for group in (to_across, to_up, to_down, share, share_across, share_down, share_up):
         for copy in group:
             copy.wait_send()
     pltpu.make_async_copy(parts.at[1], parts.at[1], part_send).wait()
     pltpu.make_async_copy(parts.at[0, 1], parts.at[0, 1], part_send).wait()
-    pltpu.make_async_copy(parts.at[0, 0, 0, 0], parts.at[0, 0, 0, 0], part_send).wait()
-    if ys > 1:
-        sent = parts.at[0, 0, pl.ds(1, ys - 1)]
-        pltpu.make_async_copy(sent, sent, part_send).wait()
+    sent = parts.at[0, 0, pl.ds(1, owners - 1)]
+    pltpu.make_async_copy(sent, sent, part_send).wait()
 
 
 def body(qkv_in, short_taps, long_filter, skip_gain, out_weight):
@@ -543,9 +543,11 @@
             pltpu.VMEM(exchange, BF16),
             pltpu.VMEM((blocks * CH, rows), F32),
             pltpu.VMEM((zs, 2, columns, channels), BF16),
-            pltpu.VMEM((2 * rows, half), BF16),
-            pltpu.VMEM((2, 2, 2 * rows, channels), BF16),
-            pltpu.VMEM((2, 2, ys, 2, wide, rows), BF16),
+            pltpu.VMEM((half, 2 * rows), F32),
+            pltpu.VMEM((half, 2 * rows), F32),
+            pltpu.VMEM((2, 2, 2, zs, 2 * CH, 2 * rows), BF16),
+            pltpu.VMEM((2, 2, channels, 2 * rows), BF16),
+            pltpu.VMEM((2, 2, 2 * ys, wide, rows), BF16),
             pltpu.VMEM((8, ys, wide, rows), BF16),
             dma((9,)),
             dma((5,)),
@@ -556,8 +558,8 @@
             dma((zs,)),
             dma((zs,)),
             dma((zs,)),
-            dma((7, 2)),
-            dma((7, 2)),
+            dma((7, 4)),
+            dma((7, 4)),
             dma,
             dma((8, ys)),
         ],

time: 76.7 us -> 76.8 us (level)
  the two profiles are of different devices: /device:TPU:1 before, /device:TPU:15 now
where the time goes in v6:
time: 76.8 us; the launch traced here: 76.7 us
  Pallas kernels  75.1 us (98%)
  local copies, waits for them, and re-layouts  1.57 us (2%)
    pallas_call x1, Pallas kernels, body(): pl.pallas_call(mixer_kernel, out_shape=jax.ShapeDtypeStruct((rows, channe...  75.1 us
    unnamed x1, local copies, waits for them, and re-layouts  1.57 us

profile of v6, /device:TPU:15, one launch (start us, length us, event | category | flops | bytes accessed | tf_op | source)
XLA Modules:
  0.0 76.7 jit_solution(2595367736240283113)
XLA Ops:
  0.0 75.1 %mixer.1 = bf16[128,512]{1,0:T(8,128)(2,1)} custom-call(bf16[3,128,512]{2,1,0:T(8,128)(2,1)} %bitcast.3, f32[3,3,512]{2,1,0:T(4,128)} %taps_hbm.1, f32[128,512]{1,0:T(8,128)} %filt_hbm.1, f32[1,512]{1,0:T(1,128)} %bitcast.5, bf16[64,512]{1,0:T(8,128)(2,1)} %bitcast.4, f32[128,64]{1,0:T(8,128)} %constant.8.clone.a_fwd_hbm, ...), custom_call_target="tpu_custom_call" | custom-call | tf_op jit(solution)/shard_map/mixer/pallas_call | solution.py:522
  75.1 1.6 %copy.11 = bf16[128,512]{1,0:T(8,128)(2,1)} copy(bf16[128,512]{1,0:T(8,128)(2,1)} %mixer.1) | data formatting | bytes 262144

commit v7 on v6

--- a/solution.py
+++ b/solution.py
@@ -248,45 +248,47 @@
     right_steps = zs // 2
     left_steps = zs - 1 - right_steps
 
-    def pass_on(block, step, send_sem, recv_sem, ahead):
+    def pass_on(block, lane, step, send_sem, recv_sem, ahead):
+        half_block = weight.at[block, lax.rem(xl + lane, 2)]
         return pltpu.make_async_remote_copy(
-            src_ref=weight.at[block],
-            dst_ref=weight.at[block],
-            send_sem=send_sem.at[step],
-            recv_sem=recv_sem.at[step],
+            src_ref=half_block,
+            dst_ref=half_block,
+            send_sem=send_sem.at[lane, step],
+            recv_sem=recv_sem.at[lane, step],
             device_id={"z": lax.rem(z + ahead, zs)},
         )
 
-    def right_copy(step):
-        return pass_on(lax.rem(z + zs - step, zs), step, right_send, right_recv, 1)
-
-    def left_copy(step):
-        return pass_on(lax.rem(z + step, zs), step, left_send, left_recv, zs - 1)
-
-    def landing(step, shift, sem):
-        landed_at = weight.at[lax.rem(z + shift, zs)]
-        pltpu.make_async_copy(landed_at, landed_at, sem.at[step]).wait()
-
-    def ring(step):
+    def right_copy(lane, step):
+        return pass_on(lax.rem(z + zs - step, zs), lane, step, right_send, right_recv, 1)
+
+    def left_copy(lane, step):
+        return pass_on(lax.rem(z + step, zs), lane, step, left_send, left_recv, zs - 1)
+
+    def landing(lane, step, shift, sem):
+        landed_at = weight.at[lax.rem(z + shift, zs), lax.rem(xl + lane, 2)]
+        pltpu.make_async_copy(landed_at, landed_at, sem.at[lane, step]).wait()
+
+    def ring(lane, step):
         if step > right_steps:
             return
-        if step == 0:
+        if step == 0 and lane == 0:
             weight_load.wait()
+        if step == 0 and lane == 1:
             swap.wait_recv()
         if 0 < step <= right_steps:
-            landing(step - 1, zs - step, right_recv)
+            landing(lane, step - 1, zs - step, right_recv)
         if 0 < step <= left_steps:
-            landing(step - 1, step, left_recv)
+            landing(lane, step - 1, step, left_recv)
         if step < right_steps:
-            right_copy(step).start()
+            right_copy(lane, step).start()
         if step < left_steps:
-            left_copy(step).start()
-
+            left_copy(lane, step).start()
+
+    ring(0, 0)
     h_pair[:, my_rows, :] = h_own[pl.ds(core, 1)].reshape(chips, CH, rows)
     h_copy.wait_recv()
     h_send[...] = h_pair[...].astype(BF16)
     send_all(z, xh, h_send, h_recv, far_send.at[0], far_recv.at[0])
-    ring(0)
 
     x_load.wait()
     small[0].wait()
@@ -306,7 +308,8 @@
     flipped = mixed_in.T.reshape(chips, CH, 2 * rows)
     u_send[...] = jnp.concatenate([flipped[:, :, :rows], flipped[:, :, rows:]], axis=1).astype(BF16)
     send_all(z, xh, u_send, u_recv, far_send.at[1], far_recv.at[1])
-    ring(1)
+    ring(1, 0)
+    ring(0, 1)
     query_t[...] = query.T
     skip_t[...] = (skip[:, mine] * mixed_in).T
 
@@ -317,15 +320,19 @@
     b_dft[...] = jnp.concatenate([high, high, low], axis=0)
     high, low = high_low(a_back[...])
     a_inv[...] = jnp.concatenate([high, high, low], axis=1)
+    ring(1, 1)
     for group in range(4):
         wait_group(h_recv, far_recv.at[0], group)
-    ring(2)
+        if group == 1:
+            ring(0, 2)
+    ring(1, 2)
     t_re, t_im = t_both[0], t_both[1]
     h_freq = spectrum(h_recv, scratch, a_fwd, t_re, t_im, b_dft)
     for group in range(4):
         wait_group(u_recv, far_recv.at[1], group)
         if group == 1:
-            ring(3)
+            ring(0, 3)
+            ring(1, 3)
     u_freq = spectrum(u_recv, scratch, a_fwd, t_re, t_im, b_dft)
     width = t_re.shape[1]
     h_re, h_im = h_freq[:, :width], h_freq[:, width:]
@@ -334,7 +341,8 @@
     inverse(product, scratch, t_re, t_im, b_dft, a_inv)
     y_send[...] = scratch[...].reshape(y_send.shape).astype(BF16)
     send_all(z, xh, y_send, y_recv, far_send.at[2], far_recv.at[2], by_turn=True)
-    ring(4)
+    ring(0, 4)
+    ring(1, 4)
 
     tokens = 2 * rows
     turns = zs // 4
@@ -378,14 +386,17 @@
         to_up[group].start()
         to_down[group].start()
         share[group].start()
-        if group == 1:
-            ring(5)
-    ring(6)
+        if group % 2 == 0:
+            ring(0, 5 + group // 2)
+            ring(1, 5 + group // 2)
     for group in range(4):
         to_up[group].wait_recv()
         share_down[group].start()
         to_down[group].wait_recv()
         share_up[group].start()
+    ring(0, 7)
+    ring(1, 7)
+    for group in range(4):
         to_across[group].wait_recv()
         share_across[group].start()
 
@@ -400,20 +411,9 @@
                     shift = lax.rem(z + zs - block, zs) - zs // 2
                     turn = jnp.where(shift < 0, -2 * shift - 1, 2 * shift)
                     start = c * half + block * pairs
-                    g_ordered[which_x, part, start : start + pairs, :] = g_all[
-                        which_x, part, c, pl.ds(turn, 1)
+                    g_ordered[part, start : start + pairs, :] = g_all[
+                        pl.ds(which_x, 1), part, c, pl.ds(turn, 1)
                     ].reshape(pairs, tokens)
-
-    def compute(which_x, to):
-        product = jnp.zeros((wide, tokens), F32)
-        for part in range(2):
-            block = weight[pl.ds(to * per_owner, per_owner), part].reshape(wide, 2 * half)
-            right = g_ordered[pl.ds(which_x, 1), part].reshape(2 * half, tokens)
-            product = product + dot(block, right)
-        for b in range(2):
-            parts[pl.ds(which_x, 1), b, pl.ds(to, 1)] = (
-                product[:, b * rows : (b + 1) * rows].astype(BF16).reshape(1, 1, wide, rows)
-            )
 
     def send(which_x, b, to):
         pltpu.make_async_remote_copy(
@@ -424,12 +424,28 @@
             device_id={"xh": which_x, "xl": lax.rem(to, 2), "core": b, "y": to // 2},
         ).start()
 
-    def project(which_x, first, count):
-        def step(k, carry):
-            to = lax.rem(z // per_owner + owners + first + lax.rem(k + y, count), owners)
-            compute(which_x, to)
+    def project(which_x, own, first, count):
+        targets = [
+            lax.rem(z // per_owner + owners + first + lax.rem(y + k, count), owners)
+            for k in range(count)
+        ]
+        product = jnp.zeros((count * wide, tokens), F32)
+        for part in range(2):
+            left = [
+                weight[pl.ds(to * per_owner, per_owner), part].reshape(wide, 2 * half)
+                for to in targets
+            ]
+            product = product + dot(jnp.concatenate(left, axis=0), g_ordered[part])
+        for k, to in enumerate(targets):
             for b in range(2):
-                stays = (which_x == xh) & (b == core) & (to == owner_me)
+                value = product[k * wide : (k + 1) * wide, b * rows : (b + 1) * rows]
+                parts[pl.ds(which_x, 1), b, pl.ds(to, 1)] = value.astype(BF16).reshape(
+                    1, 1, wide, rows
+                )
+                if not own:
+                    send(which_x, b, to)
+                    continue
+                stays = (b == core) & (to == owner_me)
 
                 @pl.when(jnp.logical_not(stays))
                 def _():
@@ -441,24 +457,38 @@
                         pl.ds(which_x, 1), b, pl.ds(to, 1)
                     ].reshape(1, 1, wide, rows)
 
-            return carry
-
-        lax.fori_loop(0, count, step, 0)
-
     near = min(5, owners)
     for group in range(4):
-        for copy in (share, share_down, share_up, share_across):
-            copy[group].wait_recv()
-    order(0)
-    order(1)
-    project(1 - xh, -(near // 2), near)
-    project(xh, -(near // 2), near)
-    ring(7)
-    for step in range(8, right_steps + 1):
-        ring(step)
+        share[group].wait_recv()
+
+        @pl.when(xl == 0)
+        def _():
+            share_up[group].wait_recv()
+
+        @pl.when(xl == 1)
+        def _():
+            share_down[group].wait_recv()
+
+    order(xh)
+    project(xh, True, -(near // 2), near)
     if near < owners:
-        project(1 - xh, near - near // 2, owners - near)
-        project(xh, near - near // 2, owners - near)
+        for step in range(8, right_steps + 1):
+            ring(0, step)
+            ring(1, step)
+        project(xh, True, near - near // 2, owners - near)
+    for group in range(4):
+        share_across[group].wait_recv()
+
+        @pl.when(xl == 1)
+        def _():
+            share_up[group].wait_recv()
+
+        @pl.when(xl == 0)
+        def _():
+            share_down[group].wait_recv()
+
+    order(1 - xh)
+    project(1 - xh, False, -(owners // 2), owners)
 
     def arrived(k, carry):
         index = lax.rem(my_index + k, everyone)
@@ -492,9 +522,11 @@
 
     swap.wait_send()
     for step in range(right_steps):
-        right_copy(step).wait_send()
+        for lane in range(2):
+            right_copy(lane, step).wait_send()
     for step in range(left_steps):
-        left_copy(step).wait_send()
+        for lane in range(2):
+            left_copy(lane, step).wait_send()
     wait_blocks(chips - 1, h_send, far_send.at[0])
     wait_blocks(chips - 1, u_send, far_send.at[1])
     wait_blocks(chips - 1, y_send, far_send.at[2])
@@ -546,7 +578,7 @@
             pltpu.VMEM((half, 2 * rows), F32),
             pltpu.VMEM((half, 2 * rows), F32),
             pltpu.VMEM((2, 2, 2, zs, 2 * CH, 2 * rows), BF16),
-            pltpu.VMEM((2, 2, channels, 2 * rows), BF16),
+            pltpu.VMEM((2, channels, 2 * rows), BF16),
             pltpu.VMEM((2, 2, 2 * ys, wide, rows), BF16),
             pltpu.VMEM((8, ys, wide, rows), BF16),
             dma((9,)),
@@ -554,10 +586,10 @@
             dma((4,)),
             dma((3,)),
             dma((3, 4)),
-            dma((zs,)),
-            dma((zs,)),
-            dma((zs,)),
-            dma((zs,)),
+            dma((2, zs)),
+            dma((2, zs)),
+            dma((2, zs)),
+            dma((2, zs)),
             dma((7, 4)),
             dma((7, 4)),
             dma,

time: 76.8 us -> 76.3 us (level)
  the two profiles are of different devices: /device:TPU:15 before, /device:TPU:1 now
where the time goes in v7:
time: 76.3 us; the launch traced here: 76.1 us
  Pallas kernels  74.6 us (98%)
  local copies, waits for them, and re-layouts  1.57 us (2%)
    pallas_call x1, Pallas kernels, body(): pl.pallas_call(mixer_kernel, out_shape=jax.ShapeDtypeStruct((rows, channe...  74.6 us
    unnamed x1, local copies, waits for them, and re-layouts  1.57 us

profile of v7, /device:TPU:1, one launch (start us, length us, event | category | flops | bytes accessed | tf_op | source)
XLA Modules:
  0.0 76.1 jit_solution(4852280515864691364)
XLA Ops:
  0.0 74.6 %mixer.1 = bf16[128,512]{1,0:T(8,128)(2,1)} custom-call(bf16[3,128,512]{2,1,0:T(8,128)(2,1)} %bitcast.3, f32[3,3,512]{2,1,0:T(4,128)} %taps_hbm.1, f32[128,512]{1,0:T(8,128)} %filt_hbm.1, f32[1,512]{1,0:T(1,128)} %bitcast.5, bf16[64,512]{1,0:T(8,128)(2,1)} %bitcast.4, f32[128,64]{1,0:T(8,128)} %constant.8.clone.a_fwd_hbm, ...), custom_call_target="tpu_custom_call" | custom-call | tf_op jit(solution)/shard_map/mixer/pallas_call | solution.py:554
  74.6 1.6 %copy.11 = bf16[128,512]{1,0:T(8,128)(2,1)} copy(bf16[128,512]{1,0:T(8,128)(2,1)} %mixer.1) | data formatting | bytes 262144

commit v8 on v7

--- a/solution.py
+++ b/solution.py
@@ -289,6 +289,7 @@
     h_copy.wait_recv()
     h_send[...] = h_pair[...].astype(BF16)
     send_all(z, xh, h_send, h_recv, far_send.at[0], far_recv.at[0])
+    ring(1, 0)
 
     x_load.wait()
     small[0].wait()
@@ -308,7 +309,6 @@
     flipped = mixed_in.T.reshape(chips, CH, 2 * rows)
     u_send[...] = jnp.concatenate([flipped[:, :, :rows], flipped[:, :, rows:]], axis=1).astype(BF16)
     send_all(z, xh, u_send, u_recv, far_send.at[1], far_recv.at[1])
-    ring(1, 0)
     ring(0, 1)
     query_t[...] = query.T
     skip_t[...] = (skip[:, mine] * mixed_in).T
@@ -323,16 +323,13 @@
     ring(1, 1)
     for group in range(4):
         wait_group(h_recv, far_recv.at[0], group)
-        if group == 1:
-            ring(0, 2)
-    ring(1, 2)
     t_re, t_im = t_both[0], t_both[1]
     h_freq = spectrum(h_recv, scratch, a_fwd, t_re, t_im, b_dft)
     for group in range(4):
         wait_group(u_recv, far_recv.at[1], group)
-        if group == 1:
-            ring(0, 3)
-            ring(1, 3)
+        if group == 2:
+            ring(0, 2)
+            ring(1, 2)
     u_freq = spectrum(u_recv, scratch, a_fwd, t_re, t_im, b_dft)
     width = t_re.shape[1]
     h_re, h_im = h_freq[:, :width], h_freq[:, width:]
@@ -340,6 +337,8 @@
     product = jnp.concatenate([h_re * u_im + h_im * u_re, h_re * u_re - h_im * u_im], axis=1)
     inverse(product, scratch, t_re, t_im, b_dft, a_inv)
     y_send[...] = scratch[...].reshape(y_send.shape).astype(BF16)
+    ring(0, 3)
+    ring(1, 3)
     send_all(z, xh, y_send, y_recv, far_send.at[2], far_recv.at[2], by_turn=True)
     ring(0, 4)
     ring(1, 4)
@@ -386,9 +385,9 @@
         to_up[group].start()
         to_down[group].start()
         share[group].start()
-        if group % 2 == 0:
-            ring(0, 5 + group // 2)
-            ring(1, 5 + group // 2)
+        if group in (0, 3):
+            ring(0, 5 + group // 3)
+            ring(1, 5 + group // 3)
     for group in range(4):
         to_up[group].wait_recv()
         share_down[group].start()
@@ -404,14 +403,15 @@
     owner_me = y * 2 + xl
     wide = per_owner * columns
 
-    def order(which_x):
+    def order(far):
+        which_x = 1 - xh if far else xh
         for part in range(2):
             for c in range(2):
                 for block in range(zs):
                     shift = lax.rem(z + zs - block, zs) - zs // 2
                     turn = jnp.where(shift < 0, -2 * shift - 1, 2 * shift)
                     start = c * half + block * pairs
-                    g_ordered[part, start : start + pairs, :] = g_all[
+                    g_ordered[far, part, start : start + pairs, :] = g_all[
                         pl.ds(which_x, 1), part, c, pl.ds(turn, 1)
                     ].reshape(pairs, tokens)
 
@@ -424,7 +424,8 @@
             device_id={"xh": which_x, "xl": lax.rem(to, 2), "core": b, "y": to // 2},
         ).start()
 
-    def project(which_x, own, first, count):
+    def project(far, first, count):
+        which_x = 1 - xh if far else xh
         targets = [
             lax.rem(z // per_owner + owners + first + lax.rem(y + k, count), owners)
             for k in range(count)
@@ -435,14 +436,14 @@
                 weight[pl.ds(to * per_owner, per_owner), part].reshape(wide, 2 * half)
                 for to in targets
             ]
-            product = product + dot(jnp.concatenate(left, axis=0), g_ordered[part])
+            product = product + dot(jnp.concatenate(left, axis=0), g_ordered[far, part])
         for k, to in enumerate(targets):
             for b in range(2):
                 value = product[k * wide : (k + 1) * wide, b * rows : (b + 1) * rows]
                 parts[pl.ds(which_x, 1), b, pl.ds(to, 1)] = value.astype(BF16).reshape(
                     1, 1, wide, rows
                 )
-                if not own:
+                if far:
                     send(which_x, b, to)
                     continue
                 stays = (b == core) & (to == owner_me)
@@ -469,26 +470,27 @@
         def _():
             share_down[group].wait_recv()
 
-    order(xh)
-    project(xh, True, -(near // 2), near)
+    order(0)
+    project(0, -(near // 2), near)
+    for group in range(4):
+        share_across[group].wait_recv()
+
+        @pl.when(xl == 1)
+        def _():
+            share_up[group].wait_recv()
+
+        @pl.when(xl == 0)
+        def _():
+            share_down[group].wait_recv()
+
+    order(1)
+    project(1, -(near // 2), near)
     if near < owners:
         for step in range(8, right_steps + 1):
             ring(0, step)
             ring(1, step)
-        project(xh, True, near - near // 2, owners - near)
-    for group in range(4):
-        share_across[group].wait_recv()
-
-        @pl.when(xl == 1)
-        def _():
-            share_up[group].wait_recv()
-
-        @pl.when(xl == 0)
-        def _():
-            share_down[group].wait_recv()
-
-    order(1 - xh)
-    project(1 - xh, False, -(owners // 2), owners)
+        project(1, near - near // 2, owners - near)
+        project(0, near - near // 2, owners - near)
 
     def arrived(k, carry):
         index = lax.rem(my_index + k, everyone)
@@ -578,7 +580,7 @@
             pltpu.VMEM((half, 2 * rows), F32),
             pltpu.VMEM((half, 2 * rows), F32),
             pltpu.VMEM((2, 2, 2, zs, 2 * CH, 2 * rows), BF16),
-            pltpu.VMEM((2, channels, 2 * rows), BF16),
+            pltpu.VMEM((2, 2, channels, 2 * rows), BF16),
             pltpu.VMEM((2, 2, 2 * ys, wide, rows), BF16),
             pltpu.VMEM((8, ys, wide, rows), BF16),
             dma((9,)),

time: 76.3 us -> 73.6 us (0.965)
  Pallas kernels: 74.6 us -> 71.9 us
    pallas_call x1, Pallas kernels: 74.6 us -> 71.9 us  [body(): pl.pallas_call(mixer_kernel, out_shape=jax.ShapeDtypeStruct((rows, channe...]
where the time goes in v8:
time: 73.6 us; the launch traced here: 73.5 us
  Pallas kernels  71.9 us (98%)
  local copies, waits for them, and re-layouts  1.57 us (2%)
    pallas_call x1, Pallas kernels, body(): pl.pallas_call(mixer_kernel, out_shape=jax.ShapeDtypeStruct((rows, channe...  71.9 us
    unnamed x1, local copies, waits for them, and re-layouts  1.57 us

profile of v8, /device:TPU:1, one launch (start us, length us, event | category | flops | bytes accessed | tf_op | source)
XLA Modules:
  0.0 73.5 jit_solution(4978157746972992047)
XLA Ops:
  0.0 71.9 %mixer.1 = bf16[128,512]{1,0:T(8,128)(2,1)} custom-call(bf16[3,128,512]{2,1,0:T(8,128)(2,1)} %bitcast.3, f32[3,3,512]{2,1,0:T(4,128)} %taps_hbm.1, f32[128,512]{1,0:T(8,128)} %filt_hbm.1, f32[1,512]{1,0:T(1,128)} %bitcast.5, bf16[64,512]{1,0:T(8,128)(2,1)} %bitcast.4, f32[128,64]{1,0:T(8,128)} %constant.8.clone.a_fwd_hbm, ...), custom_call_target="tpu_custom_call" | custom-call | tf_op jit(solution)/shard_map/mixer/pallas_call | solution.py:556
  71.9 1.6 %copy.11 = bf16[128,512]{1,0:T(8,128)(2,1)} copy(bf16[128,512]{1,0:T(8,128)(2,1)} %mixer.1) | data formatting | bytes 262144

commit v9 on v8

--- a/solution.py
+++ b/solution.py
@@ -37,27 +37,37 @@
     return high, (value - high.astype(F32)).astype(BF16)
 
 
-def send_all(z, xh, source, target, send_sem, recv_sems, by_turn=False):
+def hops(turn):
+    if isinstance(turn, int):
+        return -((turn + 1) // 2) if turn % 2 else turn // 2
+    return jnp.where(lax.rem(turn, 2) == 1, -((turn + 1) // 2), turn // 2)
+
+
+def send_all(z, xh, source, target, send_sem, recv_sems, near_first=False):
     zs = lax.axis_size("z")
     me = z * 2 + xh
     size = 2 * zs // recv_sems.shape[0]
 
     def step(k, carry):
         turn = k // 2
-        ahead = zs // 2 + jnp.where(lax.rem(turn, 2) == 1, -((turn + 1) // 2), turn // 2)
+        ahead = hops(turn) + (zs if near_first else zs // 2)
         to_z = lax.rem(z + ahead, zs)
         to_x = jnp.where(lax.rem(k, 2) == 0, 1 - xh, xh)
         pltpu.make_async_remote_copy(
             src_ref=source.at[to_z * 2 + to_x],
-            dst_ref=target.at[turn * 2 + xh if by_turn else me],
+            dst_ref=target.at[turn * 2 + xh if near_first else me],
             send_sem=send_sem,
             recv_sem=recv_sems.at[k // size],
             device_id={"z": to_z, "xh": to_x},
         ).start()
         return carry
 
-    lax.fori_loop(0, 2 * zs - 1, step, 0)
-    slot = (zs - 1) * 2 + xh if by_turn else me
+    if near_first:
+        step(0, 0)
+        lax.fori_loop(2, 2 * zs, step, 0)
+    else:
+        lax.fori_loop(0, 2 * zs - 1, step, 0)
+    slot = xh if near_first else me
     target[pl.ds(slot, 1)] = source[pl.ds(me, 1)]
 
 
@@ -66,9 +76,9 @@
     pltpu.make_async_copy(part, part, sem).wait()
 
 
-def wait_group(ref, sems, group):
+def wait_group(ref, sems, group, short):
     size = ref.shape[0] // sems.shape[0]
-    wait_blocks(size - (group == sems.shape[0] - 1), ref, sems.at[group])
+    wait_blocks(size - (group == short), ref, sems.at[group])
 
 
 def spectrum(received, scratch, a_fwd, t_re, t_im, b_dft):
@@ -148,6 +158,36 @@
     down_x = {"xh": down // 2, "xl": lax.rem(down, 2)}
     columns = weight.shape[2]
 
+    barrier = pltpu.get_barrier_semaphore()
+    step_to = lax.rem(me + jnp.where(core == 1, 1, chips - 1), chips)
+    pl.semaphore_signal(
+        barrier, inc=1, device_id={"z": step_to // 2, "xh": lax.rem(step_to, 2), "core": other}
+    )
+
+
+    def place_of(index):
+        which = index // ys
+        return {
+            "xh": which // 4,
+            "xl": lax.rem(which // 2, 2),
+            "core": lax.rem(which, 2),
+            "y": lax.rem(index, ys),
+        }
+
+    def greet_ctx(k, carry):
+        peer = lax.rem(me + k, chips)
+        pl.semaphore_signal(
+            barrier, inc=1, device_id={"z": peer // 2, "xh": lax.rem(peer, 2)}
+        )
+        return carry
+
+    def greet_plane(k, carry):
+        pl.semaphore_signal(barrier, inc=1, device_id=place_of(lax.rem(my_index + k, everyone)))
+        return carry
+
+    lax.fori_loop(1, chips, greet_ctx, 0)
+    lax.fori_loop(1, everyone, greet_plane, 0)
+
     filt_load = local_copy(filt_hbm, filt, load_sem.at[0])
     x_load = local_copy(qkv_hbm.at[:, :, mine], x_all.at[:, place, :], load_sem.at[1])
     weight_load = local_copy(
@@ -168,36 +208,6 @@
             ]
         )
     ]
-
-    barrier = pltpu.get_barrier_semaphore()
-    step_to = lax.rem(me + jnp.where(core == 1, 1, chips - 1), chips)
-    pl.semaphore_signal(
-        barrier, inc=1, device_id={"z": step_to // 2, "xh": lax.rem(step_to, 2), "core": other}
-    )
-
-
-    def place_of(index):
-        which = index // ys
-        return {
-            "xh": which // 4,
-            "xl": lax.rem(which // 2, 2),
-            "core": lax.rem(which, 2),
-            "y": lax.rem(index, ys),
-        }
-
-    def greet_ctx(k, carry):
-        peer = lax.rem(me + k, chips)
-        pl.semaphore_signal(
-            barrier, inc=1, device_id={"z": peer // 2, "xh": lax.rem(peer, 2)}
-        )
-        return carry
-
-    def greet_plane(k, carry):
-        pl.semaphore_signal(barrier, inc=1, device_id=place_of(lax.rem(my_index + k, everyone)))
-        return carry
-
-    lax.fori_loop(1, chips, greet_ctx, 0)
-    lax.fori_loop(1, everyone, greet_plane, 0)
 
     filt_load.wait()
     h_own[...] = filt[...].T.reshape(2, chips, CH, rows)
@@ -322,12 +332,12 @@
     a_inv[...] = jnp.concatenate([high, high, low], axis=1)
     ring(1, 1)
     for group in range(4):
-        wait_group(h_recv, far_recv.at[0], group)
+        wait_group(h_recv, far_recv.at[0], group, 3)
     t_re, t_im = t_both[0], t_both[1]
     h_freq = spectrum(h_recv, scratch, a_fwd, t_re, t_im, b_dft)
     for group in range(4):
-        wait_group(u_recv, far_recv.at[1], group)
-        if group == 2:
+        wait_group(u_recv, far_recv.at[1], group, 3)
+        if group == 0:
             ring(0, 2)
             ring(1, 2)
     u_freq = spectrum(u_recv, scratch, a_fwd, t_re, t_im, b_dft)
@@ -337,9 +347,9 @@
     product = jnp.concatenate([h_re * u_im + h_im * u_re, h_re * u_re - h_im * u_im], axis=1)
     inverse(product, scratch, t_re, t_im, b_dft, a_inv)
     y_send[...] = scratch[...].reshape(y_send.shape).astype(BF16)
+    send_all(z, xh, y_send, y_recv, far_send.at[2], far_recv.at[2], near_first=True)
     ring(0, 3)
     ring(1, 3)
-    send_all(z, xh, y_send, y_recv, far_send.at[2], far_recv.at[2], by_turn=True)
     ring(0, 4)
     ring(1, 4)
 
@@ -369,10 +379,10 @@
     share_down = g_copies(5, down, {"core": other})
     share_up = g_copies(6, up, {"core": other})
     for group in range(4):
-        wait_group(y_recv, far_recv.at[2], group)
+        wait_group(y_recv, far_recv.at[2], group, 0)
         for turn in range(group * turns, (group + 1) * turns):
-            ahead = zs // 2 + (-((turn + 1) // 2) if turn % 2 else turn // 2)
-            source = pl.ds(pl.multiple_of(lax.rem(z + zs - ahead, zs) * pairs, pairs), pairs)
+            origin = lax.rem(z + zs - hops(turn), zs)
+            source = pl.ds(pl.multiple_of(origin * pairs, pairs), pairs)
             back = y_recv[pl.ds(2 * turn, 2)].astype(F32)
             convolved = jnp.concatenate(
                 [back[:, CH * b : CH * (b + 1), :].reshape(pairs, rows) for b in range(2)], axis=1
@@ -385,7 +395,7 @@
         to_up[group].start()
         to_down[group].start()
         share[group].start()
-        if group in (0, 3):
+        if group in (1, 3):
             ring(0, 5 + group // 3)
             ring(1, 5 + group // 3)
     for group in range(4):
@@ -408,7 +418,8 @@
         for part in range(2):
             for c in range(2):
                 for block in range(zs):
-                    shift = lax.rem(z + zs - block, zs) - zs // 2
+                    shift = lax.rem(z + zs - block, zs)
+                    shift = jnp.where(shift < zs // 2, shift, shift - zs)
                     turn = jnp.where(shift < 0, -2 * shift - 1, 2 * shift)
                     start = c * half + block * pairs
                     g_ordered[far, part, start : start + pairs, :] = g_all[
@@ -458,7 +469,7 @@
                         pl.ds(which_x, 1), b, pl.ds(to, 1)
                     ].reshape(1, 1, wide, rows)
 
-    near = min(5, owners)
+    near = min(7, owners)
     for group in range(4):
         share[group].wait_recv()
 

time: 73.6 us -> 70.9 us (0.963)
  Pallas kernels: 71.9 us -> 69 us
    pallas_call x1, Pallas kernels: 71.9 us -> 69 us  [body(): pl.pallas_call(mixer_kernel, out_shape=jax.ShapeDtypeStruct((rows, channe...]
where the time goes in v9:
time: 70.9 us; the launch traced here: 70.5 us
  Pallas kernels  69 us (97%)
  local copies, waits for them, and re-layouts  1.57 us (2%)
    pallas_call x1, Pallas kernels, body(): pl.pallas_call(mixer_kernel, out_shape=jax.ShapeDtypeStruct((rows, channe...  69 us
    unnamed x1, local copies, waits for them, and re-layouts  1.57 us

profile of v9, /device:TPU:1, one launch (start us, length us, event | category | flops | bytes accessed | tf_op | source)
XLA Modules:
  0.0 70.5 jit_solution(13776535655321609495)
XLA Ops:
  0.0 69.0 %mixer.1 = bf16[128,512]{1,0:T(8,128)(2,1)} custom-call(bf16[3,128,512]{2,1,0:T(8,128)(2,1)} %bitcast.3, f32[3,3,512]{2,1,0:T(4,128)} %taps_hbm.1, f32[128,512]{1,0:T(8,128)} %filt_hbm.1, f32[1,512]{1,0:T(1,128)} %bitcast.5, bf16[64,512]{1,0:T(8,128)(2,1)} %bitcast.4, f32[128,64]{1,0:T(8,128)} %constant.8.clone.a_fwd_hbm, ...), custom_call_target="tpu_custom_call" | custom-call | tf_op jit(solution)/shard_map/mixer/pallas_call | solution.py:567
  69.0 1.6 %copy.11 = bf16[128,512]{1,0:T(8,128)(2,1)} copy(bf16[128,512]{1,0:T(8,128)(2,1)} %mixer.1) | data formatting | bytes 262144

commit v10 on v9

--- a/solution.py
+++ b/solution.py
@@ -63,8 +63,9 @@
         return carry
 
     if near_first:
+        lax.fori_loop(2 * zs - size, 2 * zs, step, 0)
         step(0, 0)
-        lax.fori_loop(2, 2 * zs, step, 0)
+        lax.fori_loop(2, 2 * zs - size, step, 0)
     else:
         lax.fori_loop(0, 2 * zs - 1, step, 0)
     slot = xh if near_first else me
@@ -210,18 +211,10 @@
     ]
 
     filt_load.wait()
-    h_own[...] = filt[...].T.reshape(2, chips, CH, rows)
+    turned = filt[...].T.reshape(2, chips, CH, rows)
+    h_send[...] = jnp.concatenate([turned[0], turned[1]], axis=1).astype(BF16)
     pl.semaphore_wait(barrier, 1 + chips - 1 + everyone - 1)
 
-    my_rows = pl.ds(pl.multiple_of(core * CH, CH), CH)
-    h_copy = pltpu.make_async_remote_copy(
-        src_ref=h_own.at[other],
-        dst_ref=h_pair.at[:, my_rows, :],
-        send_sem=near_send.at[0],
-        recv_sem=near_recv.at[0],
-        device_id={"core": other},
-    )
-    h_copy.start()
     x_copy = pltpu.make_async_remote_copy(
         src_ref=qkv_hbm.at[:, :, theirs],
         dst_ref=x_all.at[:, place, :],
@@ -246,6 +239,8 @@
     def _():
         halo_copy(0).start()
         halo_copy(1).start()
+
+    send_all(z, xh, h_send, h_recv, far_send.at[0], far_recv.at[0])
 
     swap = pltpu.make_async_remote_copy(
         src_ref=weight_hbm.at[pl.ds(pl.multiple_of((1 - xl) * columns, columns), columns), :],
@@ -295,10 +290,6 @@
             left_copy(lane, step).start()
 
     ring(0, 0)
-    h_pair[:, my_rows, :] = h_own[pl.ds(core, 1)].reshape(chips, CH, rows)
-    h_copy.wait_recv()
-    h_send[...] = h_pair[...].astype(BF16)
-    send_all(z, xh, h_send, h_recv, far_send.at[0], far_recv.at[0])
     ring(1, 0)
 
     x_load.wait()
@@ -306,21 +297,23 @@
     small[1].wait()
     x_copy.wait_recv()
     halo_copy(0).wait_recv()
-    features = []
-    for s in range(3):
-        raw = x_all[s].astype(F32)
+
+    def feature(kind):
+        raw = x_all[kind].astype(F32)
         first = jnp.where(me == 0, 0.0, raw[:halo])
         raw = jnp.concatenate([first, raw[halo:]], axis=0)
-        total = taps[s, 0:1, mine] * raw[halo:]
+        total = taps[kind, 0:1, mine] * raw[halo:]
         for back in range(1, taps.shape[1]):
-            total = total + taps[s, back : back + 1, mine] * raw[halo - back : halo - back + 2 * rows]
-        features.append(total)
-    query, mixed_in = features[0], features[1] * features[2]
+            shifted = raw[halo - back : halo - back + 2 * rows]
+            total = total + taps[kind, back : back + 1, mine] * shifted
+        return total
+
+    mixed_in = feature(1) * feature(2)
     flipped = mixed_in.T.reshape(chips, CH, 2 * rows)
     u_send[...] = jnp.concatenate([flipped[:, :, :rows], flipped[:, :, rows:]], axis=1).astype(BF16)
     send_all(z, xh, u_send, u_recv, far_send.at[1], far_recv.at[1])
     ring(0, 1)
-    query_t[...] = query.T
+    query_t[...] = feature(0).T
     skip_t[...] = (skip[:, mine] * mixed_in).T
 
     for load in small[2:]:
@@ -333,8 +326,21 @@
     ring(1, 1)
     for group in range(4):
         wait_group(h_recv, far_recv.at[0], group, 3)
+    my_rows = pl.ds(pl.multiple_of(core * CH, CH), CH)
+    their_rows = pl.ds(pl.multiple_of(other * CH, CH), CH)
+    h_own[...] = h_recv[...].astype(F32)
+    h_copy = pltpu.make_async_remote_copy(
+        src_ref=h_own.at[:, their_rows, :],
+        dst_ref=h_pair.at[:, my_rows, :],
+        send_sem=near_send.at[0],
+        recv_sem=near_recv.at[0],
+        device_id={"core": other},
+    )
+    h_copy.start()
+    h_pair[:, my_rows, :] = h_own[:, my_rows, :]
+    h_copy.wait_recv()
     t_re, t_im = t_both[0], t_both[1]
-    h_freq = spectrum(h_recv, scratch, a_fwd, t_re, t_im, b_dft)
+    h_freq = spectrum(h_pair, scratch, a_fwd, t_re, t_im, b_dft)
     for group in range(4):
         wait_group(u_recv, far_recv.at[1], group, 3)
         if group == 0:
@@ -395,16 +401,16 @@
         to_up[group].start()
         to_down[group].start()
         share[group].start()
-        if group in (1, 3):
-            ring(0, 5 + group // 3)
-            ring(1, 5 + group // 3)
+        if group == 3:
+            ring(0, 5)
+            ring(1, 5)
     for group in range(4):
         to_up[group].wait_recv()
         share_down[group].start()
         to_down[group].wait_recv()
         share_up[group].start()
-    ring(0, 7)
-    ring(1, 7)
+    ring(0, 6)
+    ring(1, 6)
     for group in range(4):
         to_across[group].wait_recv()
         share_across[group].start()
@@ -469,7 +475,7 @@
                         pl.ds(which_x, 1), b, pl.ds(to, 1)
                     ].reshape(1, 1, wide, rows)
 
-    near = min(7, owners)
+    near, nearer = min(7, owners), min(5, owners)
     for group in range(4):
         share[group].wait_recv()
 
@@ -482,7 +488,9 @@
             share_down[group].wait_recv()
 
     order(0)
-    project(0, -(near // 2), near)
+    project(0, -(nearer // 2), nearer)
+    ring(0, 7)
+    ring(1, 7)
     for group in range(4):
         share_across[group].wait_recv()
 
@@ -496,12 +504,13 @@
 
     order(1)
     project(1, -(near // 2), near)
+    for step in range(8, right_steps + 1):
+        ring(0, step)
+        ring(1, step)
     if near < owners:
-        for step in range(8, right_steps + 1):
-            ring(0, step)
-            ring(1, step)
         project(1, near - near // 2, owners - near)
-        project(0, near - near // 2, owners - near)
+    if nearer < owners:
+        project(0, nearer - nearer // 2, owners - nearer)
 
     def arrived(k, carry):
         index = lax.rem(my_index + k, everyone)
@@ -577,7 +586,7 @@
             pltpu.VMEM((2 * blocks, 2 * blocks), BF16),
             pltpu.VMEM((6 * rows, 2 * rows), BF16),
             pltpu.VMEM((blocks, 6 * blocks), BF16),
-            pltpu.VMEM((2, chips, CH, rows), F32),
+            pltpu.VMEM(exchange, F32),
             pltpu.VMEM(exchange, F32),
             pltpu.VMEM(exchange, BF16),
             pltpu.VMEM(exchange, BF16),

time: 70.9 us -> 69 us (0.973)
  Pallas kernels: 69 us -> 67.1 us
    pallas_call x1, Pallas kernels: 69 us -> 67.1 us  [body(): pl.pallas_call(mixer_kernel, out_shape=jax.ShapeDtypeStruct((rows, channe...]
where the time goes in v10:
time: 69 us; the launch traced here: 68.6 us
  Pallas kernels  67.1 us (97%)
  local copies, waits for them, and re-layouts  1.57 us (2%)
    pallas_call x1, Pallas kernels, body(): pl.pallas_call(mixer_kernel, out_shape=jax.ShapeDtypeStruct((rows, channe...  67.1 us
    unnamed x1, local copies, waits for them, and re-layouts  1.57 us

profile of v10, /device:TPU:1, one launch (start us, length us, event | category | flops | bytes accessed | tf_op | source)
XLA Modules:
  0.0 68.6 jit_solution(8054060045149017232)
XLA Ops:
  0.0 67.1 %mixer.1 = bf16[128,512]{1,0:T(8,128)(2,1)} custom-call(bf16[3,128,512]{2,1,0:T(8,128)(2,1)} %bitcast.3, f32[3,3,512]{2,1,0:T(4,128)} %taps_hbm.1, f32[128,512]{1,0:T(8,128)} %filt_hbm.1, f32[1,512]{1,0:T(1,128)} %bitcast.5, bf16[64,512]{1,0:T(8,128)(2,1)} %bitcast.4, f32[128,64]{1,0:T(8,128)} %constant.8.clone.a_fwd_hbm, ...), custom_call_target="tpu_custom_call" | custom-call | tf_op jit(solution)/shard_map/mixer/pallas_call | solution.py:576
  67.1 1.6 %copy.11 = bf16[128,512]{1,0:T(8,128)(2,1)} copy(bf16[128,512]{1,0:T(8,128)(2,1)} %mixer.1) | data formatting | bytes 262144

commit v11 on v10

--- a/solution.py
+++ b/solution.py
@@ -356,8 +356,6 @@
     send_all(z, xh, y_send, y_recv, far_send.at[2], far_recv.at[2], near_first=True)
     ring(0, 3)
     ring(1, 3)
-    ring(0, 4)
-    ring(1, 4)
 
     tokens = 2 * rows
     turns = zs // 4
@@ -401,9 +399,9 @@
         to_up[group].start()
         to_down[group].start()
         share[group].start()
-        if group == 3:
-            ring(0, 5)
-            ring(1, 5)
+        if group in (0, 3):
+            ring(0, 4 + group // 3)
+            ring(1, 4 + group // 3)
     for group in range(4):
         to_up[group].wait_recv()
         share_down[group].start()

time: 69 us -> 68.4 us (level)
  no operation moved by 1% of the time
where the time goes in v11:
time: 68.4 us; the launch traced here: 68.3 us
  Pallas kernels  66.7 us (98%)
  local copies, waits for them, and re-layouts  1.57 us (2%)
    pallas_call x1, Pallas kernels, body(): pl.pallas_call(mixer_kernel, out_shape=jax.ShapeDtypeStruct((rows, channe...  66.7 us
    unnamed x1, local copies, waits for them, and re-layouts  1.57 us

profile of v11, /device:TPU:1, one launch (start us, length us, event | category | flops | bytes accessed | tf_op | source)
XLA Modules:
  0.0 68.3 jit_solution(2843177993228959866)
XLA Ops:
  0.0 66.7 %mixer.1 = bf16[128,512]{1,0:T(8,128)(2,1)} custom-call(bf16[3,128,512]{2,1,0:T(8,128)(2,1)} %bitcast.3, f32[3,3,512]{2,1,0:T(4,128)} %taps_hbm.1, f32[128,512]{1,0:T(8,128)} %filt_hbm.1, f32[1,512]{1,0:T(1,128)} %bitcast.5, bf16[64,512]{1,0:T(8,128)(2,1)} %bitcast.4, f32[128,64]{1,0:T(8,128)} %constant.8.clone.a_fwd_hbm, ...), custom_call_target="tpu_custom_call" | custom-call | tf_op jit(solution)/shard_map/mixer/pallas_call | solution.py:574
  66.7 1.6 %copy.11 = bf16[128,512]{1,0:T(8,128)(2,1)} copy(bf16[128,512]{1,0:T(8,128)(2,1)} %mixer.1) | data formatting | bytes 262144

commit v12 on v11

--- a/solution.py
+++ b/solution.py
@@ -417,18 +417,17 @@
     owner_me = y * 2 + xl
     wide = per_owner * columns
 
-    def order(far):
+    def order(far, part):
         which_x = 1 - xh if far else xh
-        for part in range(2):
-            for c in range(2):
-                for block in range(zs):
-                    shift = lax.rem(z + zs - block, zs)
-                    shift = jnp.where(shift < zs // 2, shift, shift - zs)
-                    turn = jnp.where(shift < 0, -2 * shift - 1, 2 * shift)
-                    start = c * half + block * pairs
-                    g_ordered[far, part, start : start + pairs, :] = g_all[
-                        pl.ds(which_x, 1), part, c, pl.ds(turn, 1)
-                    ].reshape(pairs, tokens)
+        for c in range(2):
+            for block in range(zs):
+                shift = lax.rem(z + zs - block, zs)
+                shift = jnp.where(shift < zs // 2, shift, shift - zs)
+                turn = jnp.where(shift < 0, -2 * shift - 1, 2 * shift)
+                start = c * half + block * pairs
+                g_ordered[far, pl.ds(part, 1), start : start + pairs, :] = g_all[
+                    pl.ds(which_x, 1), pl.ds(part, 1), c, pl.ds(turn, 1)
+                ].reshape(1, pairs, tokens)
 
     def send(which_x, b, to):
         pltpu.make_async_remote_copy(
@@ -476,6 +475,8 @@
     near, nearer = min(7, owners), min(5, owners)
     for group in range(4):
         share[group].wait_recv()
+    order(0, xl)
+    for group in range(4):
 
         @pl.when(xl == 0)
         def _():
@@ -485,13 +486,11 @@
         def _():
             share_down[group].wait_recv()
 
-    order(0)
+    order(0, 1 - xl)
     project(0, -(nearer // 2), nearer)
     ring(0, 7)
     ring(1, 7)
     for group in range(4):
-        share_across[group].wait_recv()
-
         @pl.when(xl == 1)
         def _():
             share_up[group].wait_recv()
@@ -500,7 +499,10 @@
         def _():
             share_down[group].wait_recv()
 
-    order(1)
+    order(1, 1 - xl)
+    for group in range(4):
+        share_across[group].wait_recv()
+    order(1, xl)
     project(1, -(near // 2), near)
     for step in range(8, right_steps + 1):
         ring(0, step)

time: 68.4 us -> 68.4 us (level)
  no operation moved by 1% of the time
where the time goes in v12:
time: 68.4 us; the launch traced here: 68.2 us
  Pallas kernels  66.6 us (97%)
  local copies, waits for them, and re-layouts  1.57 us (2%)
    pallas_call x1, Pallas kernels, body(): pl.pallas_call(mixer_kernel, out_shape=jax.ShapeDtypeStruct((rows, channe...  66.6 us
    unnamed x1, local copies, waits for them, and re-layouts  1.57 us

profile of v12, /device:TPU:1, one launch (start us, length us, event | category | flops | bytes accessed | tf_op | source)
XLA Modules:
  0.0 68.2 jit_solution(2698793467996014693)
XLA Ops:
  0.0 66.6 %mixer.1 = bf16[128,512]{1,0:T(8,128)(2,1)} custom-call(bf16[3,128,512]{2,1,0:T(8,128)(2,1)} %bitcast.3, f32[3,3,512]{2,1,0:T(4,128)} %taps_hbm.1, f32[128,512]{1,0:T(8,128)} %filt_hbm.1, f32[1,512]{1,0:T(1,128)} %bitcast.5, bf16[64,512]{1,0:T(8,128)(2,1)} %bitcast.4, f32[128,64]{1,0:T(8,128)} %constant.8.clone.a_fwd_hbm, ...), custom_call_target="tpu_custom_call" | custom-call | tf_op jit(solution)/shard_map/mixer/pallas_call | solution.py:576
  66.6 1.6 %copy.11 = bf16[128,512]{1,0:T(8,128)(2,1)} copy(bf16[128,512]{1,0:T(8,128)(2,1)} %mixer.1) | data formatting | bytes 262144
